TPU v7x, 128 devices: a whole 4x4x4 slice. The times are simulated.
128 devices in a mesh: ctx: 32 (over y, x, core), grp: 4 (over z).
Axes of the slice: x: 4, y: 4, z: 4, core: 2. Of those that a mesh axis runs over, the one named last changes fastest.
Arguments:
- query_rows: bfloat16 [32768, 1024], P(('ctx', 'grp')), may hold values from -6 to 6
- key_rows: bfloat16 [32768, 1024], P(('ctx', 'grp')), may hold values from -6 to 6
- value_rows: bfloat16 [32768, 2048], P(('ctx', 'grp')), may hold values from -6 to 6
- log_decay: float32 [16, 32768], P(None, ('ctx', 'grp')), may hold values from -2 to 0, as said below
- beta_logit: float32 [16, 32768], P(None, ('ctx', 'grp')), may hold values from -8 to 6
- grad_out: bfloat16 [32768, 2048], P(('ctx', 'grp')), may hold values from -6 to 6
Outputs:
- layer_out: float32 [32768, 2048], P(('ctx', 'grp'))
- grad_query: float32 [32768, 1024], P(('ctx', 'grp'))
- grad_key: float32 [32768, 1024], P(('ctx', 'grp'))
- grad_value: float32 [32768, 2048], P(('ctx', 'grp'))
- grad_decay: float32 [16, 32768], P(None, ('ctx', 'grp'))
- grad_beta: float32 [16, 32768], P(None, ('ctx', 'grp'))
Inputs may be any that keep to these rules, and one draw needn't show every extreme that they name: `log_decay`: every entry is negative.
All inputs are finite; a program needn't handle non-finite values.
Results may differ from a plain program's by a relative error of at most 0.00035.
Values sent between devices are 32-bit elements; how exact they have to be, the bound alone decides.
A program may use at most 192 MiB of HBM per device.

v0:
```python
import jax
import jax.numpy as jnp
from jax import lax
from jax.sharding import PartitionSpec as P

DK = 128
DV = 128
VALUE_HEADS_HALF = 16
KEY_HEADS = 8


exact_mode = lax.Precision.HIGHEST


def from_behind(block, axis, distance):
    devices = range(lax.axis_size(axis))
    route = [(i - distance, i) for i in devices if i - distance in devices]
    return lax.ppermute(block, axis, route)


def entering_2(value, axis, join, neutral, backward):
    count, mine = (lax.axis_size(axis), lax.axis_index(axis))
    pieces = jax.tree.map(lambda part: lax.all_gather(part, axis), value)
    if backward:
        pieces = jax.tree.map(lambda part: part[::-1], pieces)
        mine = count - 1 - mine
    total = jax.tree.map(
        lambda part, zero: jnp.full_like(part, 0) + jnp.asarray(zero, part.dtype), value, neutral
    )

    def lap(position, total):
        longer = join(total, jax.tree.map(lambda part: part[position], pieces))
        return jax.tree.map(lambda new, old: jnp.where(position < mine, new, old), longer, total)

    return lax.fori_loop(0, count - 1, lap, total)


def from_root(shard, axis, root):
    mine = lax.axis_index(axis) == root
    return lax.psum(jnp.where(mine, shard, jnp.zeros_like(shard)), axis)


def contract(pattern, former, latter):
    return jnp.einsum(pattern, former, latter, precision=exact_mode)


def unit_heads(matrix, heads_in, head_size):
    length = matrix.shape[0]
    shaped = matrix.reshape(length, heads_in, head_size)
    shaped = shaped * lax.rsqrt(jnp.sum(shaped * shaped, axis=-1, keepdims=True) + 1e-06)
    shaped = jnp.repeat(shaped, VALUE_HEADS_HALF // heads_in, axis=1)
    return shaped.transpose(1, 0, 2)


def prepare(query_part, key_part, value_part, rate_part, gate_part):
    length = query_part.shape[0]
    queries_n = unit_heads(query_part, KEY_HEADS, DK)
    keys_n = unit_heads(key_part, KEY_HEADS, DK)
    values_h = value_part.reshape(length, VALUE_HEADS_HALF, DV).transpose(1, 0, 2)
    strength = jax.nn.sigmoid(gate_part)
    running = jnp.cumsum(rate_part, axis=1)
    row_index = lax.broadcasted_iota(jnp.int32, (length, length), 0)
    column_index = lax.broadcasted_iota(jnp.int32, (length, length), 1)
    within = row_index >= column_index
    before = row_index > column_index
    spread = running[:, :, None] - running[:, None, :]
    decay_within = jnp.where(within, jnp.exp(jnp.where(within, spread, 0.0)), 0.0)
    decay_before = jnp.where(before, decay_within, 0.0)
    system = strength[:, :, None] * decay_before * contract("htd,hsd->hts", keys_n, keys_n)
    system = system + jnp.eye(length, dtype=jnp.float32)
    mixing = contract("htd,hsd->hts", queries_n, keys_n) * decay_within
    return (queries_n, keys_n, values_h, strength, running, system, mixing)


def block_step(query_part, key_part, value_part, rate_part, gate_part, carried):
    length = query_part.shape[0]
    queries_n, keys_n, values_h, strength, running, system, mixing = prepare(
        query_part, key_part, value_part, rate_part, gate_part
    )
    growth = jnp.exp(running)
    target = strength[:, :, None] * (
        values_h - growth[:, :, None] * contract("htd,hde->hte", keys_n, carried)
    )
    written = jax.scipy.linalg.solve_triangular(system, target, lower=True, unit_diagonal=True)
    outputs = growth[:, :, None] * contract("htd,hde->hte", queries_n, carried) + contract(
        "hts,hse->hte", mixing, written
    )
    fading = jnp.exp(running[:, -1:] - running)
    final_state = growth[:, -1][:, None, None] * carried + contract(
        "hsd,hse->hde", fading[:, :, None] * keys_n, written
    )
    return (outputs.transpose(1, 0, 2).reshape(length, VALUE_HEADS_HALF * DV), final_state)


def transitions(query_part, key_part, value_part, rate_part, gate_part, grad_heads):
    queries_n, keys_n, values_h, strength, running, system, mixing = prepare(
        query_part, key_part, value_part, rate_part, gate_part
    )
    growth = jnp.exp(running)
    target = jnp.concatenate(
        [strength[:, :, None] * values_h, (strength * growth)[:, :, None] * keys_n], axis=2
    )
    solved = jax.scipy.linalg.solve_triangular(system, target, lower=True, unit_diagonal=True)
    written = solved[:, :, :DV]
    leakage = solved[:, :, DV:]
    fading = jnp.exp(running[:, -1:] - running)
    faded_keys = fading[:, :, None] * keys_n
    identity_block = jnp.eye(DK, dtype=jnp.float32)
    forward_trans = growth[:, -1][:, None, None] * identity_block - contract(
        "hsd,hsf->hdf", faded_keys, leakage
    )
    forward_offset = contract("hsd,hse->hde", faded_keys, written)
    reached = contract("hts,hte->hse", mixing, grad_heads)
    backward_offset = contract(
        "htd,hte->hde", growth[:, :, None] * queries_n, grad_heads
    ) - contract("hsd,hse->hde", leakage, reached)
    return ((forward_trans, forward_offset), (forward_trans.transpose(0, 2, 1), backward_offset))


def compose(earlier, latter):
    return (
        contract("hij,hjk->hik", latter[0], earlier[0]),
        contract("hij,hjk->hik", latter[0], earlier[1]) + latter[1],
    )


def apply_pair(pair_in, incoming):
    return contract("hij,hjk->hik", pair_in[0], incoming) + pair_in[1]


def neutral(heads_here):
    return (
        jnp.broadcast_to(jnp.eye(DK, dtype=jnp.float32), (heads_here, DK, DK)),
        jnp.zeros((heads_here, DK, DV), jnp.float32),
    )


def chain_groups(group_pair, backward):
    direction = -1 if backward else 1

    def advance(turn_number, incoming):
        return from_behind(apply_pair(group_pair, incoming), "ctx", direction)

    return lax.fori_loop(0, lax.axis_size("ctx") - 1, advance, jnp.zeros_like(group_pair[1]))


def carry_along(pair_in, backward):
    groups = lax.axis_size("grp")
    member = lax.axis_index("grp")
    per_member = VALUE_HEADS_HALF // groups
    before_pair = entering_2(
        (pair_in[0], pair_in[1]), "grp", compose, neutral(VALUE_HEADS_HALF), backward
    )
    through = compose(before_pair, pair_in)
    root_member = 0 if backward else groups - 1
    whole_pair = (
        from_root(through[0], "grp", root_member),
        from_root(through[1], "grp", root_member),
    )
    own_share = (
        lax.dynamic_slice_in_dim(whole_pair[0], member * per_member, per_member, 0),
        lax.dynamic_slice_in_dim(whole_pair[1], member * per_member, per_member, 0),
    )
    entering = chain_groups(own_share, backward)
    group_state = lax.all_gather(entering, "grp", axis=0, tiled=True)
    return apply_pair(before_pair, group_state)


def on_device(query_rows, key_rows, value_rows, log_decay, beta_logit, grad_out):
    query_float = query_rows.astype(jnp.float32)
    key_float = key_rows.astype(jnp.float32)
    value_float = value_rows.astype(jnp.float32)
    grad_float = grad_out.astype(jnp.float32)
    length = query_float.shape[0]
    grad_heads = grad_float.reshape(length, VALUE_HEADS_HALF, DV).transpose(1, 0, 2)
    forward_pair, backward_pair = transitions(
        query_float, key_float, value_float, log_decay, beta_logit, grad_heads
    )
    state_in = carry_along(forward_pair, False)
    grad_end = carry_along(backward_pair, True)

    def local_layer(query_part, key_part, value_part, rate_part, gate_part):
        return block_step(query_part, key_part, value_part, rate_part, gate_part, state_in)

    primal, pullback = jax.vjp(
        local_layer, query_float, key_float, value_float, log_decay, beta_logit
    )
    gradients = pullback((grad_float, grad_end))
    return (primal[0], gradients[0], gradients[1], gradients[2], gradients[3], gradients[4])


def solution(mesh):
    in_specs = (
        P(("ctx", "grp"), None),
        P(("ctx", "grp"), None),
        P(("ctx", "grp"), None),
        P(None, ("ctx", "grp")),
        P(None, ("ctx", "grp")),
        P(("ctx", "grp"), None),
    )
    out_specs = (
        P(("ctx", "grp"), None),
        P(("ctx", "grp"), None),
        P(("ctx", "grp"), None),
        P(("ctx", "grp"), None),
        P(None, ("ctx", "grp")),
        P(None, ("ctx", "grp")),
    )
    return jax.shard_map(
        on_device, mesh=mesh, in_specs=in_specs, out_specs=out_specs, check_vma=False
    )
```

profile of v0, /device:TPU:0, one launch (start us, length us, event | category | flops | bytes accessed | tf_op | source)
XLA Modules:
  0.0 1629.9 jit_solution(17556664244587411370)
XLA Ops:
  21.2 10.1 while.57
  31.4 315.8 %custom-call.10 = f32[16,2,128,128]{2,3,1,0:T(8,128)} custom-call(f32[16,2,128,128]{3,2,1,0:T(8,128)} %bitcast.287), custom_call_target="InvertDiagBlocksLowerTriangular" | custom-call | tf_op jit(solution)/shard_map/jit(_solve_triangular)/vmap()/triangular_solve | solution.py:103
  410.4 30.1 %all-gather.21.cloned.1.call-done = f32[64,128,128]{2,1,0:T(8,128)} async-done(((f32[16,128,128]{2,1,0:T(8,128)}), f32[64,128,128]{2,1,0:T(8,128)}) %all-gather.21.cloned.1.call-update) | async-done | bytes 4194320 | tf_op jit(solution)/shard_map/all_gather | solution.py:23
  445.2 45.7 %all-gather.19.cloned.1.call-done = f32[64,128,128]{2,1,0:T(8,128)} async-done(((f32[16,128,128]{2,1,0:T(8,128)}), f32[64,128,128]{2,1,0:T(8,128)}) %all-gather.19.cloned.1.call-update) | async-done | bytes 4194320 | tf_op jit(solution)/shard_map/all_gather | solution.py:23
  495.7 17.1 %while.59 = (s32[]{:T(128)}, f32[16,128,128]{2,1,0:T(8,128)S(1)}, f32[16,128,128]{2,1,0:T(8,128)S(1)}, s32[]{:T(128)}, f32[4,16,128,128]{3,2,1,0:T(8,128)}, /*in...) while((s32[]{:T(128)}, f32[16,128,128]{2,1,0:T(8,128)S(1)}, f32[16,128,128]{2,1,0:T(8,128)S(1)}, ...), condition=%wide.region_13.14_spmd.clone, body=%wide.region_12.13_spmd.clone.sunk | while | flops 806617088 | bytes 13634664 | solution.py:35
  518.8 23.0 %all-gather.17.cloned.1.call-done = f32[64,128,128]{2,1,0:T(8,128)} async-done(((f32[16,128,128]{2,1,0:T(8,128)}), f32[64,128,128]{2,1,0:T(8,128)}) %all-gather.17.cloned.1.call-update) | async-done | bytes 4194320 | tf_op jit(solution)/shard_map/all_gather | solution.py:23
  541.8 50.8 %all-gather.15.cloned.1.call-done = f32[64,128,128]{2,1,0:T(8,128)} async-done(((f32[16,128,128]{2,1,0:T(8,128)}), f32[64,128,128]{2,1,0:T(8,128)}) %all-gather.15.cloned.1.call-update) | async-done | bytes 4194320 | tf_op jit(solution)/shard_map/all_gather | solution.py:23
  592.7 16.4 %while.58 = (s32[]{:T(128)}, f32[16,128,128]{2,1,0:T(8,128)S(1)}, f32[16,128,128]{2,1,0:T(8,128)S(1)}, s32[]{:T(128)}, f32[4,16,128,128]{3,2,1,0:T(8,128)}, /*in...) while((s32[]{:T(128)}, f32[16,128,128]{2,1,0:T(8,128)S(1)}, f32[16,128,128]{2,1,0:T(8,128)S(1)}, ...), condition=%wide.region_5.6_spmd.clone, body=%wide.region_4.5_spmd.clone.sunk | while | flops 806617088 | bytes 13634664 | solution.py:35
  616.6 93.9 %all-reduce.5.cloned.1.call-done = (f32[16,128,128]{2,1,0:T(8,128)}, f32[16,128,128]{2,1,0:T(8,128)}, f32[16,128,128]{2,1,0:T(8,128)}, f32[16,128,128]{2,1,0:T(8,128)}) async-done(((f32[16,128,128]{2,1,0:T(8,128)}, f32[16,128,128]{2,1,0:T(8,128)}, f32[16,128,128]{2,1,0:T(8,128)}, f32[16,128,128]{2,1,0:T(8,128)}), (f32[16,128,128]{2,1,0:T(8,128)}, f32[16,128,128]{2,1,0:T(8,128)}, f32[16,128,128]{2,1,0:T(8,128)}, ...) | async-done | bytes 4194320 | tf_op jit(solution)/shard_map/psum | solution.py:40
  717.2 337.1 %while.55 = (s32[]{:T(128)}, f32[4,128,128]{2,1,0:T(8,128)S(1)}, f32[4,128,128]{2,1,0:T(8,128)}, f32[4,128,128]{2,1,0:T(8,128)}, s32[]{:T(128)}) while((s32[]{:T(128)}, f32[4,128,128]{2,1,0:T(8,128)S(1)}, f32[4,128,128]{2,1,0:T(8,128)}, f32[4,128,128]{2,1,0:T(8,128)}, s32[]{:T(128)}) %tuple.170), condition=%wide.region_9.10_spmd, body=%wide.region_8.9_spmd.sunk | while | flops 100728832 | bytes 2097253 | solution.py:144
  1055.1 377.9 %while.56 = (s32[]{:T(128)}, f32[4,128,128]{2,1,0:T(8,128)S(1)}, f32[4,128,128]{2,1,0:T(8,128)}, f32[4,128,128]{2,1,0:T(8,128)}, s32[]{:T(128)}) while((s32[]{:T(128)}, f32[4,128,128]{2,1,0:T(8,128)S(1)}, f32[4,128,128]{2,1,0:T(8,128)}, f32[4,128,128]{2,1,0:T(8,128)}, s32[]{:T(128)}) %tuple.173), condition=%wide.region_17.18_spmd, body=%wide.region_16.17_spmd.sunk | while | flops 100728832 | bytes 2097253 | solution.py:144
  1070.5 9.3 collective-permute-done.1
  1095.3 9.4 collective-permute-done.1
  1108.1 9.0 collective-permute-done.1
  1120.4 9.4 collective-permute-done.1
  1145.2 8.9 collective-permute-done.1
  1157.6 8.7 collective-permute-done.1
  1181.8 8.7 collective-permute-done.1
  1193.9 8.7 collective-permute-done.1
  1218.2 8.7 collective-permute-done.1
  1230.3 8.7 collective-permute-done.1
  1254.6 8.7 collective-permute-done.1
  1290.9 8.7 collective-permute-done.1
  1327.3 8.7 collective-permute-done.1
  1339.4 8.7 collective-permute-done.1
  1363.7 8.7 collective-permute-done.1
  1400.0 8.7 collective-permute-done.1
  1437.1 54.3 %all-gather.13.cloned.1.call-done = f32[16,128,128]{2,1,0:T(8,128)} async-done(((f32[4,128,128]{2,1,0:T(8,128)}), f32[16,128,128]{2,1,0:T(8,128)}) %all-gather.13.cloned.1.call-update) | async-done | bytes 1048592 | tf_op jit(solution)/shard_map/all_gather | solution.py:165
  1523.2 11.3 multiply_reduce_fusion
  1534.5 9.6 fusion.73
  1559.4 9.2 fusion.37
  1603.9 8.9 bitcast_add_fusion.4
  (450 shorter events, 818.5 us)
Async XLA Ops:
  7.2 433.3 %all-gather.21.cloned.1.call-start = ((), (), s32[]{:S(2)}) async-start(), calls=%async_computation.5 | async-start | bytes 5242880 | tf_op jit(solution)/shard_map/all_gather | solution.py:23
  389.4 101.5 %all-gather.19.cloned.1.call-start = ((), (), s32[]{:S(2)}) async-start(), calls=%async_computation.4 | async-start | bytes 5242880 | tf_op jit(solution)/shard_map/all_gather | solution.py:23
  402.2 139.6 %all-gather.17.cloned.1.call-start = ((), (), s32[]{:S(2)}) async-start(), calls=%async_computation.3 | async-start | bytes 5242880 | tf_op jit(solution)/shard_map/all_gather | solution.py:23
  408.8 183.8 %all-gather.15.cloned.1.call-start = ((), (), s32[]{:S(2)}) async-start(), calls=%async_computation.2 | async-start | bytes 5242880 | tf_op jit(solution)/shard_map/all_gather | solution.py:23
  410.2 300.3 %all-reduce.5.cloned.1.call-start = ((), (), s32[]{:S(2)}) async-start(), calls=%async_computation.6 | async-start | bytes 8388608 | tf_op jit(solution)/shard_map/psum | solution.py:40
  616.5 817.2 %all-gather.11.cloned.1.call-start = ((), (), s32[]{:S(2)}) async-start(), calls=%async_computation | async-start | bytes 1310720 | tf_op jit(solution)/shard_map/all_gather | solution.py:165
  874.6 10.0 collective-permute-start
  886.7 10.0 collective-permute-start
  910.9 10.0 collective-permute-start
  923.1 10.0 collective-permute-start
  947.3 10.0 collective-permute-start
  959.4 10.0 collective-permute-start
  971.6 10.0 collective-permute-start
  995.8 10.0 collective-permute-start
  1007.9 10.0 collective-permute-start
  1020.0 10.0 collective-permute-start
  1032.2 10.0 collective-permute-start
  1055.0 436.4 %all-gather.13.cloned.1.call-start = ((), (), s32[]{:S(2)}) async-start(), calls=%async_computation.1 | async-start | bytes 1310720 | tf_op jit(solution)/shard_map/all_gather | solution.py:165
  1069.2 10.6 collective-permute-start.1
  1094.0 10.7 collective-permute-start.1
  1106.8 10.3 collective-permute-start.1
  1119.2 10.7 collective-permute-start.1
  1143.9 10.2 collective-permute-start.1
  1156.3 10.0 collective-permute-start.1
  1180.5 10.0 collective-permute-start.1
  1216.9 10.0 collective-permute-start.1
  1253.3 10.0 collective-permute-start.1
  1289.6 10.0 collective-permute-start.1
  1326.0 10.0 collective-permute-start.1
  1338.1 10.0 collective-permute-start.1
  1362.4 10.0 collective-permute-start.1
  1398.8 10.0 collective-permute-start.1
  (96 other events, 936.5 us)
Sparse Core Ops, SparseCore 0:
  389.5 50.9 all-gather.20
  442.2 48.6 all-gather.18
  493.1 48.6 all-gather.16
  543.9 48.6 all-gather.14
  616.7 93.8 all-reduce.4
  1055.1 60.3 all-gather.10
  1433.8 57.4 all-gather.12
where the time goes:
time: 1640 us; the launch traced here: 1630 us
  waiting for transfers between devices  611 us (37%)
  other arithmetic  343 us (21%)
  matrix products  320 us (20%)
  starting transfers between devices  269 us (16%)
  local copies, waits for them, and re-layouts  68.5 us (4%)
    another operation x5, other arithmetic, transitions(): jax.scipy.linalg.solve_triangular(system, target, lower=True, unit_diagon...  317 us
    ppermute x62, waiting for transfers between devices, from_behind(): return lax.ppermute(block, axis, route)  313 us
    dot_general x99, matrix products, contract(): return jnp.einsum(pattern, former, latter, precision=exact_mode)  291 us
    ppermute x62, starting transfers between devices, from_behind(): return lax.ppermute(block, axis, route)  269 us
    all_gather x4, waiting for transfers between devices, entering_2(): pieces = jax.tree.map(lambda part: lax.all_gather(part, axis), value)  150 us
    psum x1, waiting for transfers between devices, from_root(): return lax.psum(jnp.where(mine, shard, jnp.zeros_like(shard)), axis)  93.9 us
    all_gather x2, waiting for transfers between devices, carry_along(): group_state = lax.all_gather(entering, 'grp', axis=0, tiled=True)  54.3 us
  transfers between devices with their start and end apart: 69, of which 68 were waited for; matrix products, arithmetic and copies ran while one was open for 7% of the time, Pallas kernels for 0%

commit v1 on v0

v1 whole, which is shorter than its diff:
```python
import functools
import jax
import jax.numpy as jnp
from jax import lax
from jax.experimental import pallas as pl
from jax.experimental.pallas import tpu as pltpu
from jax.sharding import PartitionSpec as P

F32 = jnp.float32
BF16 = jnp.bfloat16
TOK = 256
D = 128
HEADS = 16
KHEADS = 8


def dg(a, b, ca, cb):
    return lax.dot_general(a, b, (((ca,), (cb,)), ((), ())), preferred_element_type=F32)


def split(x):
    hi = x.astype(BF16)
    return hi, (x - hi.astype(F32)).astype(BF16)


def dot3(a, b, ca, cb):
    return dg(a[0], b[0], ca, cb) + (dg(a[0], b[1], ca, cb) + dg(a[1], b[0], ca, cb))


def dot2l(a, b, ca, cb):
    return dg(a[0], b, ca, cb) + dg(a[1], b, ca, cb)


def dot2r(a, b, ca, cb):
    return dg(a, b[0], ca, cb) + dg(a, b[1], ca, cb)


def iota(shape, dim):
    return lax.broadcasted_iota(jnp.int32, shape, dim)


def cumulate(rows, tri):
    hi = rows.astype(BF16)
    rest = rows - hi.astype(F32)
    mid = rest.astype(BF16)
    low = (rest - mid.astype(F32)).astype(BF16)
    parts = jnp.concatenate([hi.astype(F32), mid.astype(F32), low.astype(F32), jnp.zeros((2, TOK), F32)], axis=0)
    got = dg(parts.astype(BF16), tri, 1, 0)
    return got[0:2] + (got[2:4] + got[4:6])


def invert(systems):
    n = len(systems)
    lane = iota((16, D), 1)
    row = iota((16, D), 0)
    block = lane // 16
    packed = []
    for mat in systems:
        got = jnp.where(block == 0, mat[0:16], 0.0)
        for i in range(1, 8):
            got = jnp.where(block == i, mat[16 * i : 16 * i + 16], got)
        packed.append(got)
    inv = [jnp.where(lane % 16 == row, 1.0, 0.0).astype(F32) for _ in range(n)]
    for m in range(15):
        index = block * 16 + m
        for c in range(n):
            column = jnp.take_along_axis(packed[c], index, axis=1, mode="promise_in_bounds")
            inv[c] = inv[c] - column * inv[c][m : m + 1, :]
    wide_r = iota((D, D), 0)
    wide_c = iota((D, D), 1)
    full = [
        jnp.concatenate([jnp.where(block == i, inv[c], 0.0) for i in range(8)], axis=0)
        for c in range(n)
    ]
    for b in (16, 32, 64):
        mask = (wide_r // (2 * b) == wide_c // (2 * b)) & (wide_r // b % 2 == 1) & (wide_c // b % 2 == 0)
        sides = [split(jnp.where(mask, systems[c], 0.0)) for c in range(n)]
        ts = [split(full[c]) for c in range(n)]
        inner = [split(dot3(sides[c], ts[c], 1, 0)) for c in range(n)]
        full = [full[c] - dot3(ts[c], inner[c], 1, 0) for c in range(n)]
    return full


def rows_to_cols(rows8):
    return jnp.concatenate([rows8] * 16, axis=0).T


def cols_to_rows(cols):
    lane = iota((TOK, D), 1)
    got = jnp.zeros((TOK, D), F32)
    for i, col in enumerate(cols):
        got = jnp.where(lane == i, col, got)
    return got.T


def phase1(q_ref, k_ref, v_ref, go_ref, ld_ref, bl_ref,
           tri_ref, t_ref, m_ref, gam_ref, u_ref, w_ref, r_ref, auxc_ref, end_ref):
    q = q_ref[...]
    k = k_ref[...]
    qf = q.astype(F32)
    kf = k.astype(F32)
    rq = lax.rsqrt(jnp.sum(qf * qf, axis=1, keepdims=True) + 1e-6)
    rk = lax.rsqrt(jnp.sum(kf * kf, axis=1, keepdims=True) + 1e-6)
    rk_row = cols_to_rows([rk])[0:1]
    t_i = iota((TOK, TOK), 0)
    s_i = iota((TOK, TOK), 1)
    upper = jnp.where(t_i <= s_i, 1.0, 0.0).astype(BF16)
    run = cumulate(ld_ref[0], upper)
    logit = bl_ref[0]
    beta_rows = 1.0 / (1.0 + jnp.exp(-logit))
    last = run[:, TOK - 1 : TOK]
    cols = rows_to_cols(jnp.concatenate([run, beta_rows, jnp.exp(run), jnp.exp(last - run)], axis=0))
    kk = dg(k, k, 1, 1)
    qk = dg(q, k, 1, 1)
    lane = iota((TOK, D), 1)
    auxc = jnp.where(lane == 8, rq, jnp.where(lane == 9, rk, cols))
    auxc_ref[0] = auxc
    within = t_i >= s_i
    systems = []
    for j in range(2):
        spread = jnp.where(within, cols[:, j : j + 1] - run[j : j + 1], -1e30)
        gam = jnp.exp(spread) * rk_row
        gam_ref[j] = gam
        mix = split(qk * gam * rq)
        m_ref[j, 0] = mix[0]
        m_ref[j, 1] = mix[1]
        sysm = jnp.where(t_i > s_i, kk * gam * (cols[:, 2 + j : 3 + j] * rk), 0.0)
        systems.append(sysm)
    blocks = []
    for j in range(2):
        blocks += [systems[j][:D, :D], systems[j][D:, D:]]
    inv = invert(blocks)
    eye = jnp.where(iota((D, D), 0) == iota((D, D), 1), 1.0, 0.0)
    for j in range(2):
        t11, t22 = inv[2 * j], inv[2 * j + 1]
        inner = dot3(split(systems[j][D:, :D]), split(t11), 1, 0)
        t21 = -dot3(split(t22), split(inner), 1, 0)
        whole = jnp.concatenate(
            [jnp.concatenate([t11, jnp.zeros((D, D), F32)], axis=1), jnp.concatenate([t21, t22], axis=1)], axis=0)
        tb = split(whole * beta_rows[j : j + 1])
        t_ref[j, 0] = tb[0]
        t_ref[j, 1] = tb[1]
        g = cols[:, 4 + j : 5 + j]
        f = cols[:, 6 + j : 7 + j]
        v = v_ref[:, j * D : (j + 1) * D]
        go = go_ref[:, j * D : (j + 1) * D]
        u = dot2l(tb, v, 1, 0)
        w = dot3(tb, split(kf * (g * rk)), 1, 0)
        ws = split(w)
        u_ref[j] = u
        w_ref[j, 0] = ws[0]
        w_ref[j, 1] = ws[1]
        frk = f * rk
        mix = (m_ref[j, 0], m_ref[j, 1])
        r = dot2l(mix, go, 0, 0)
        r_ref[j] = r
        whole_g = jnp.exp(last[j : j + 1])
        tri_ref[j, 0] = eye * whole_g - dot2r(k, split(w * frk), 0, 0)
        tri_ref[j, 1] = dot2l(split(u * frk), k, 0, 0)
        tri_ref[j, 2] = dot2l(split(go.astype(F32) * (g * rq)), q, 0, 0) - dot3(split(r), ws, 0, 0)
        end_ref[j] = jnp.broadcast_to(whole_g, (8, D))


def phase3(q_ref, k_ref, v_ref, go_ref, bl_ref, sg_ref, t_ref, m_ref, gam_ref, u_ref, w_ref, r_ref, auxc_ref, end_ref,
           out_ref, gq_ref, gk_ref, gv_ref, gd_ref, gb_ref):
    q = q_ref[...]
    k = k_ref[...]
    aux = auxc_ref[0]
    rq = aux[:, 8:9]
    rk = aux[:, 9:10]
    t_i = iota((TOK, TOK), 0)
    s_i = iota((TOK, TOK), 1)
    strict = t_i > s_i
    lower = jnp.where(t_i >= s_i, 1.0, 0.0).astype(BF16)
    eq = jnp.zeros((TOK, D), F32)
    ek = jnp.zeros((TOK, D), F32)
    dots = []
    ends = []
    for j in range(2):
        g = aux[:, 4 + j : 5 + j]
        f = aux[:, 6 + j : 7 + j]
        st = sg_ref[j, 0]
        gt = sg_ref[j, 1]
        ss = split(st)
        gs = split(gt)
        v = v_ref[:, j * D : (j + 1) * D]
        go = go_ref[:, j * D : (j + 1) * D]
        tb = (t_ref[j, 0], t_ref[j, 1])
        mix = (m_ref[j, 0], m_ref[j, 1])
        w = (w_ref[j, 0], w_ref[j, 1])
        frk = f * rk
        x = u_ref[j] - dot3(w, ss, 1, 1)
        xs = split(x)
        out = dot2r(q, ss, 1, 1) * (g * rq) + dot3(mix, xs, 1, 0)
        out_ref[:, j * D : (j + 1) * D] = out
        dx = r_ref[j] + dot2r(k, gs, 1, 1) * frk
        y = dot3(tb, split(dx), 0, 0)
        ys = split(y)
        gv_ref[:, j * D : (j + 1) * D] = y
        gam = gam_ref[j]
        p = split(jnp.where(strict, dot3(ys, xs, 1, 1) * gam * (-rk), 0.0))
        n = split(dot2r(go, xs, 1, 1) * gam * rq)
        eq += dot2l(n, k, 1, 0) + dot2r(go, ss, 1, 0) * (g * rq)
        ek += dot2l(p, k, 1, 0) + dot2l(p, k, 0, 0) + dot2l(n, q, 0, 0)
        ek += dot3(xs, gs, 1, 0) * frk - dot3(ys, ss, 1, 0) * (g * rk)
        dots.append(jnp.sum(go.astype(F32) * out - v.astype(F32) * y, axis=1, keepdims=True))
        dots.append(jnp.sum(y * x, axis=1, keepdims=True))
        st_end = st * end_ref[j][0:1] + dot2l(split(x * frk), k, 0, 0)
        ends.append(jnp.sum(gt * st_end, keepdims=True))
    rows = cols_to_rows([dots[0], dots[2], dots[1], dots[3]])
    suffix = cumulate(rows[0:2], lower)
    gd_ref[0] = suffix + jnp.concatenate(ends, axis=0)
    gb_ref[0] = jnp.exp(-bl_ref[0]) * rows[2:4]
    qf = q.astype(F32)
    kf = k.astype(F32)
    gq_ref[...] = eq - qf * (rq * rq * jnp.sum(qf * eq, axis=1, keepdims=True))
    gk_ref[...] = ek - kf * (rk * rk * jnp.sum(kf * ek, axis=1, keepdims=True))


def wide(width):
    return pl.BlockSpec((TOK, width), lambda i: (0, i))


def whole_spec():
    return pl.BlockSpec((1, 2, TOK), lambda i: (i, 0, 0))


def per_head(*shape):
    return pl.BlockSpec((2,) + shape, lambda i: (i,) + (0,) * len(shape))


SAVED = [
    ((2, TOK, TOK), BF16),
    ((2, TOK, TOK), BF16),
    ((TOK, TOK), F32),
    ((TOK, D), F32),
    ((2, TOK, D), BF16),
    ((TOK, D), F32),
]
AUX_SPEC = pl.BlockSpec((1, TOK, D), lambda i: (i, 0, 0))
PARAMS = dict(vmem_limit_bytes=56 * 1024 * 1024)


def run_phase1(q, k, v, go, ld, bl):
    return pl.pallas_call(
        phase1,
        grid=(KHEADS,),
        in_specs=[wide(D), wide(D), wide(2 * D), wide(2 * D), whole_spec(), whole_spec()],
        out_specs=[per_head(3, D, D)] + [per_head(*s) for s, _ in SAVED] + [AUX_SPEC, per_head(8, D)],
        out_shape=[jax.ShapeDtypeStruct((HEADS, 3, D, D), F32)]
        + [jax.ShapeDtypeStruct((HEADS,) + s, t) for s, t in SAVED]
        + [jax.ShapeDtypeStruct((KHEADS, TOK, D), F32), jax.ShapeDtypeStruct((HEADS, 8, D), F32)],
        compiler_params=pltpu.CompilerParams(**PARAMS),
        name="local_transitions",
    )(q, k, v, go, ld.reshape(KHEADS, 2, TOK), bl.reshape(KHEADS, 2, TOK))


def run_phase3(q, k, v, go, bl, sg, saved):
    *outs, gd, gb = pl.pallas_call(
        phase3,
        grid=(KHEADS,),
        in_specs=[wide(D), wide(D), wide(2 * D), wide(2 * D), whole_spec(), per_head(2, D, D)]
        + [per_head(*s) for s, _ in SAVED] + [AUX_SPEC, per_head(8, D)],
        out_specs=[wide(2 * D), wide(D), wide(D), wide(2 * D), whole_spec(), whole_spec()],
        out_shape=[
            jax.ShapeDtypeStruct((TOK, HEADS * D), F32),
            jax.ShapeDtypeStruct((TOK, KHEADS * D), F32),
            jax.ShapeDtypeStruct((TOK, KHEADS * D), F32),
            jax.ShapeDtypeStruct((TOK, HEADS * D), F32),
            jax.ShapeDtypeStruct((KHEADS, 2, TOK), F32),
            jax.ShapeDtypeStruct((KHEADS, 2, TOK), F32),
        ],
        compiler_params=pltpu.CompilerParams(**PARAMS),
        name="local_gradients",
    )(q, k, v, go, bl.reshape(KHEADS, 2, TOK), sg, *saved)
    return (*outs, gd.reshape(HEADS, TOK), gb.reshape(HEADS, TOK))


MESH = pl.DeviceIdType.MESH
NZ, NC, NX, NY = 4, 2, 4, 4
SHARE = HEADS // NZ
PAIR = SHARE // NC
HALF = D // 2


def join(early, late):
    ae, be, ce = early
    al, bl, cl = late
    als = split(al)
    cls = split(cl)
    left = (jnp.concatenate([als[0], cls[0]], axis=0), jnp.concatenate([als[1], cls[1]], axis=0))
    both = dot3(left, split(ae), 1, 0)
    return both[:D], dot3(split(be), als, 1, 1) + bl, both[D:] + ce


def join_all(parts):
    while len(parts) > 1:
        parts = [join(parts[i], parts[i + 1]) for i in range(0, len(parts), 2)]
    return parts[0]


def chain(parts, state, grad):
    split_a = [split(p[0]) for p in parts]
    states = [state]
    for i in range(len(parts) - 1):
        states.append(dot3(split(states[-1]), split_a[i], 1, 1) + parts[i][1])
    grads = [grad]
    for i in range(len(parts) - 1, 0, -1):
        grads.append(dot3(split(grads[-1]), split_a[i], 1, 0) + parts[i][2])
    return states, grads[::-1]


def scan_kernel(tri_ref, sg_ref, zin, cout, cin, xout, xin, yin, xdo, xdi, cdo, cdi, zdo,
                own, zs, zr, cs, cr, xs, xr, ys, yr, xds, xdr, cds, cdr, zds, zdr):
    ctx = lax.axis_index("ctx")
    z = lax.axis_index("grp")
    c = lax.rem(ctx, NC)
    x = lax.rem(lax.div(ctx, NC), NX)
    y = lax.div(ctx, NC * NX)
    oc = 1 - c

    def at(yy, xx, cc, zz):
        return ((yy * NX + xx) * NC + cc, zz)

    def zpeer(d):
        return lax.rem(z + d, NZ)

    def xpeer(d):
        return lax.rem(x + d, NX)

    def ypeer(d):
        return lax.rem(y + d, NY)

    barrier = pltpu.get_barrier_semaphore()
    peers = [at(y, x, c, zpeer(d)) for d in range(1, NZ)]
    peers += [at(y, x, oc, z)]
    peers += [at(y, xpeer(d), c, z) for d in range(1, NX)]
    peers += [at(ypeer(d), x, c, z) for d in range(1, NY)]
    for peer in peers:
        pl.semaphore_signal(barrier, inc=1, device_id=peer, device_id_type=MESH)
    pl.semaphore_wait(barrier, len(peers))

    def remote(src, dst, send, recv, peer):
        return pltpu.make_async_remote_copy(
            src_ref=src, dst_ref=dst, send_sem=send, recv_sem=recv, device_id=peer, device_id_type=MESH)

    def slot(i):
        return lax.rem(i + PAIR * oc, SHARE)

    def zcopy(d, i):
        to = zpeer(d)
        return remote(tri_ref.at[SHARE * to + slot(i)], zin.at[z, slot(i)], zs.at[d - 1, i], zr.at[d - 1, i],
                      at(y, x, c, to))

    mine = pltpu.make_async_copy(tri_ref.at[pl.ds(SHARE * z, SHARE)], zin.at[z], own.at[0])
    mine.start()

    def zstart(i, _):
        for d in (2, 1, 3):
            zcopy(d, i).start()
        return 0

    lax.fori_loop(0, SHARE, zstart, 0)
    mine.wait()

    def ccopy(i):
        return remote(cout.at[i], cin.at[c, i], cs.at[i], cr.at[i], at(y, x, oc, z))

    def zjoin(i):
        for d in range(1, NZ):
            zcopy(d, i).wait_recv()
        h = slot(i)
        return join_all([tuple(zin[m, h, p] for p in range(3)) for m in range(NZ)])

    def zaway(i, _):
        got = zjoin(i)
        for p in range(3):
            cout[i, p] = got[p]
        ccopy(i).start()
        return 0

    lax.fori_loop(0, PAIR, zaway, 0)

    def zhere(i, _):
        got = zjoin(i + PAIR)
        for p in range(3):
            cin[c, i, p] = got[p]
        return 0

    lax.fori_loop(0, PAIR, zhere, 0)

    for i in range(PAIR):
        ccopy(i).wait_recv()
        a, b, g = join_all([tuple(cin[m, i, p] for p in range(3)) for m in range(NC)])
        for half in range(2):
            to = 2 * i + half
            rows = slice(half * HALF, (half + 1) * HALF)
            xout[to, 0:D] = a
            xout[to, D : D + HALF] = b[rows]
            xout[to, D + HALF : 2 * D] = g[rows]

    def xcopy(d):
        return remote(xout.at[xpeer(d)], xin.at[x], xs.at[d - 1], xr.at[d - 1], at(y, xpeer(d), c, z))

    for d in (2, 1, 3):
        xcopy(d).start()
    xin[x] = xout[x]
    for d in range(1, NX):
        xcopy(d).wait_recv()

    def packed(ref, m):
        return ref[m, 0:D], ref[m, D : D + HALF], ref[m, D + HALF : 2 * D]

    row = join_all([packed(xin, m) for m in range(NX)])
    yin[y, 0:D] = row[0]
    yin[y, D : D + HALF] = row[1]
    yin[y, D + HALF : 2 * D] = row[2]

    def ycopy(d):
        return remote(yin.at[y], yin.at[y], ys.at[d - 1], yr.at[d - 1], at(ypeer(d), x, c, z))

    for d in (2, 1, 3):
        ycopy(d).start()
    for d in range(1, NY):
        ycopy(d).wait_recv()
    zero = jnp.zeros((HALF, D), F32)
    states, grads = chain([packed(yin, m) for m in range(NY)], zero, zero)
    state, grad = states[0], grads[0]
    for m in range(1, NY):
        state = jnp.where(y == m, states[m], state)
        grad = jnp.where(y == m, grads[m], grad)

    states, grads = chain([packed(xin, m) for m in range(NX)], state, grad)
    for m in range(NX):
        xdo[m, 0:HALF] = states[m]
        xdo[m, HALF:D] = grads[m]

    def xdcopy(d):
        return remote(xdo.at[xpeer(d)], xdi.at[x], xds.at[d - 1], xdr.at[d - 1], at(y, xpeer(d), c, z))

    for d in (2, 1, 3):
        xdcopy(d).start()
    xdi[x] = xdo[x]
    for d in range(1, NX):
        xdcopy(d).wait_recv()
    for i in range(PAIR):
        state = jnp.concatenate([xdi[2 * i, 0:HALF], xdi[2 * i + 1, 0:HALF]], axis=0)
        grad = jnp.concatenate([xdi[2 * i, HALF:D], xdi[2 * i + 1, HALF:D]], axis=0)
        states, grads = chain([tuple(cin[m, i, p] for p in range(3)) for m in range(NC)], state, grad)
        for m in range(NC):
            cdo[m, i, 0] = states[m]
            cdo[m, i, 1] = grads[m]

    cdcopy = remote(cdo.at[oc], cdi.at[c], cds, cdr, at(y, x, oc, z))
    cdcopy.start()
    cdi[c] = cdo[c]

    def zdcopy(d, h):
        to = zpeer(d)
        return remote(zdo.at[to, h], sg_ref.at[SHARE * z + h], zds.at[d - 1, h], zdr.at[d - 1, h], at(y, x, c, to))

    def zdown(core):
        def body(i, _):
            h = PAIR * core + i
            parts = [tuple(zin[m, h, p] for p in range(3)) for m in range(NZ)]
            states, grads = chain(parts, cdi[core, i, 0], cdi[core, i, 1])
            for m in range(NZ):
                zdo[m, h, 0] = states[m]
                zdo[m, h, 1] = grads[m]
            for d in (2, 1, 3):
                zdcopy(d, h).start()
            return 0

        lax.fori_loop(0, PAIR, body, 0)

    zdown(c)
    cdcopy.wait_recv()
    zdown(oc)
    mine = pltpu.make_async_copy(zdo.at[z], sg_ref.at[pl.ds(SHARE * z, SHARE)], own.at[1])
    mine.start()

    def zwait(i, _):
        for d in range(1, NZ):
            zcopy(d, i).wait_send()
            zdcopy(d, i).wait()
        return 0

    lax.fori_loop(0, SHARE, zwait, 0)
    for i in range(PAIR):
        ccopy(i).wait_send()
    for d in range(1, NX):
        xcopy(d).wait_send()
        xdcopy(d).wait_send()
    for d in range(1, NY):
        ycopy(d).wait_send()
    cdcopy.wait_send()
    mine.wait()


def run_scan(tri):
    dma = pltpu.SemaphoreType.DMA
    vm = lambda *shape: pltpu.VMEM(shape, F32)
    return pl.pallas_call(
        scan_kernel,
        in_specs=[pl.BlockSpec(memory_space=pl.ANY)],
        out_specs=pl.BlockSpec(memory_space=pl.ANY),
        out_shape=jax.ShapeDtypeStruct((HEADS, 2, D, D), F32),
        scratch_shapes=[
            vm(NZ, SHARE, 3, D, D), vm(PAIR, 3, D, D), vm(NC, PAIR, 3, D, D),
            vm(NX, 2 * D, D), vm(NX, 2 * D, D), vm(NY, 2 * D, D),
            vm(NX, D, D), vm(NX, D, D), vm(NC, PAIR, 2, D, D), vm(NC, PAIR, 2, D, D),
            vm(NZ, SHARE, 2, D, D),
            dma((2,)),
            dma((NZ - 1, SHARE)), dma((NZ - 1, SHARE)), dma((PAIR,)), dma((PAIR,)),
            dma((NX - 1,)), dma((NX - 1,)), dma((NY - 1,)), dma((NY - 1,)),
            dma((NX - 1,)), dma((NX - 1,)), dma, dma,
            dma((NZ - 1, SHARE)), dma((NZ - 1, SHARE)),
        ],
        compiler_params=pltpu.CompilerParams(collective_id=0, has_side_effects=True, **PARAMS),
        name="device_scan",
    )(tri)


def on_device(query_rows, key_rows, value_rows, log_decay, beta_logit, grad_out):
    tri, *saved = run_phase1(query_rows, key_rows, value_rows, grad_out, log_decay, beta_logit)
    sg = run_scan(tri)
    return run_phase3(query_rows, key_rows, value_rows, grad_out, beta_logit, sg, saved)


def solution(mesh):
    rows = P(("ctx", "grp"), None)
    heads = P(None, ("ctx", "grp"))
    return jax.shard_map(
        on_device,
        mesh=mesh,
        in_specs=(rows, rows, rows, heads, heads, rows),
        out_specs=(rows, rows, rows, rows, heads, heads),
        check_vma=False,
    )
```

time: 1640 us -> 160 us (0.10)
  waiting for transfers between devices: 611 us -> 0 us
  other arithmetic: 343 us -> 0 us
  matrix products: 320 us -> 0 us
  starting transfers between devices: 269 us -> 0 us
  Pallas kernels: 0 us -> 153 us
  local copies, waits for them, and re-layouts: 68.5 us -> 5.34 us
    another operation x11 -> x0, other arithmetic: 321 us -> none  [the longest x5 317 us: transitions(): jax.scipy.linalg.solve_triangular(system, target, lower=True, unit_diagon...]
    ppermute x62 -> x0, waiting for transfers between devices: 313 us -> none  [from_behind(): return lax.ppermute(block, axis, route)]
    dot_general x100 -> x0, matrix products: 302 us -> none  [the longest x99 291 us: contract(): return jnp.einsum(pattern, former, latter, precision=exact_mode)]
    ppermute x62 -> x0, starting transfers between devices: 269 us -> none  [from_behind(): return lax.ppermute(block, axis, route)]
    all_gather x6 -> x0, waiting for transfers between devices: 204 us -> none  [the longest x4 150 us: entering_2(): pieces = jax.tree.map(lambda part: lax.all_gather(part, axis), value)]
    pallas_call x0 -> x3, Pallas kernels: none -> 153 us  [the longest x1 90.7 us: run_scan(): pl.pallas_call(scan_kernel, in_specs=[pl.BlockSpec(memory_space=pl.ANY)],...]
    psum x1 -> x0, waiting for transfers between devices: 93.9 us -> none  [from_root(): return lax.psum(jnp.where(mine, shard, jnp.zeros_like(shard)), axis)]
    another operation x9 -> x0, matrix products: 18 us -> none  [the longest x6 9.41 us: block_step(): jax.scipy.linalg.solve_triangular(system, target, lower=True, unit_diagon...]
  transfers between devices with their start and end apart: 69 -> 0, of which waited for: 68 -> 0; matrix products, arithmetic and copies ran while one was open for 7% -> 0% of each run, Pallas kernels for 0% -> 0%
where the time goes in v1:
time: 160 us; the launch traced here: 159 us
  Pallas kernels  153 us (96%)
  local copies, waits for them, and re-layouts  5.34 us (3%)
    pallas_call x1, Pallas kernels, run_scan(): pl.pallas_call(scan_kernel, in_specs=[pl.BlockSpec(memory_space=pl.ANY)],...  90.7 us
    pallas_call x1, Pallas kernels, run_phase1(): pl.pallas_call(phase1, grid=(KHEADS,), in_specs=[wide(D), wide(D), wide(2...  33 us
    pallas_call x1, Pallas kernels, run_phase3(): pl.pallas_call(phase3, grid=(KHEADS,), in_specs=[wide(D), wide(D), wide(2...  29.4 us

profile of v1, /device:TPU:0, one launch (start us, length us, event | category | flops | bytes accessed | tf_op | source)
XLA Modules:
  0.0 159.2 jit_solution(4591082210143957578)
XLA Ops:
  0.6 1.3 reshape.25.bl_ref
  2.0 1.3 reshape.26.ld_ref
  3.3 33.0 %local_transitions.1 = (f32[16,3,128,128]{3,2,1,0:T(8,128)}, bf16[16,2,256,256]{3,2,1,0:T(8,128)(2,1)}, bf16[16,2,256,256]{3,2,1,0:T(8,128)(2,1)}, f32[16,256,25...) custom-call(bf16[256,1024]{1,0:T(8,128)(2,1)} %q_ref.3, ...), custom_call_target="tpu_custom_call" | custom-call | tf_op jit(solution)/shard_map/local_transitions/pallas_call | solution.py:245
  36.3 90.7 %device_scan.1.sg_ref = f32[16,2,128,128]{3,2,1,0:T(8,128)} custom-call(f32[16,3,128,128]{3,2,1,0:T(8,128)} %get-tuple-element.21.tri_ref), custom_call_target="tpu_custom_call" | custom-call | tf_op jit(solution)/shard_map/device_scan/pallas_call | solution.py:503
  127.0 29.4 %local_gradients.1 = (f32[256,2048]{1,0:T(8,128)}, f32[256,1024]{1,0:T(8,128)}, f32[256,1024]{1,0:T(8,128)}, f32[256,2048]{1,0:T(8,128)}, f32[8,2,256]{2,1,0:T(2,128)}, /*index=5*/f32[8,2,256]{2,1,0:T(2,128)}) custom-call(bf16[256,1024]{1,0:T(8,128)(2,1)} %q_ref.3, bf16[256,1024]{1,0:T(8,128)(2,1)} %k_ref.3, bf16[256,2048]{1,0:T(8,128)(2,1)} %v_ref.3, ...), custom_call_target="tpu_custom_call" | custom-call | tf_op jit(solution)/shard_map/local_gradients/pallas_call | solution.py:259
  156.5 1.3 reshape.27
  157.8 1.3 reshape.28

commit v2 on v1

--- a/solution.py
+++ b/solution.py
@@ -1,4 +1,3 @@
-import functools
 import jax
 import jax.numpy as jnp
 from jax import lax
@@ -93,6 +92,9 @@
     return got.T
 
 
+VMEM_LIMIT = 60 * 1024 * 1024
+
+
 def phase1(q_ref, k_ref, v_ref, go_ref, ld_ref, bl_ref,
            tri_ref, t_ref, m_ref, gam_ref, u_ref, w_ref, r_ref, auxc_ref, end_ref):
     q = q_ref[...]
@@ -105,8 +107,8 @@
     t_i = iota((TOK, TOK), 0)
     s_i = iota((TOK, TOK), 1)
     upper = jnp.where(t_i <= s_i, 1.0, 0.0).astype(BF16)
-    run = cumulate(ld_ref[0], upper)
-    logit = bl_ref[0]
+    run = cumulate(ld_ref[...], upper)
+    logit = bl_ref[...]
     beta_rows = 1.0 / (1.0 + jnp.exp(-logit))
     last = run[:, TOK - 1 : TOK]
     cols = rows_to_cols(jnp.concatenate([run, beta_rows, jnp.exp(run), jnp.exp(last - run)], axis=0))
@@ -114,7 +116,7 @@
     qk = dg(q, k, 1, 1)
     lane = iota((TOK, D), 1)
     auxc = jnp.where(lane == 8, rq, jnp.where(lane == 9, rk, cols))
-    auxc_ref[0] = auxc
+    auxc_ref[...] = auxc
     within = t_i >= s_i
     systems = []
     for j in range(2):
@@ -165,7 +167,7 @@
            out_ref, gq_ref, gk_ref, gv_ref, gd_ref, gb_ref):
     q = q_ref[...]
     k = k_ref[...]
-    aux = auxc_ref[0]
+    aux = auxc_ref[...]
     rq = aux[:, 8:9]
     rk = aux[:, 9:10]
     t_i = iota((TOK, TOK), 0)
@@ -209,71 +211,12 @@
         ends.append(jnp.sum(gt * st_end, keepdims=True))
     rows = cols_to_rows([dots[0], dots[2], dots[1], dots[3]])
     suffix = cumulate(rows[0:2], lower)
-    gd_ref[0] = suffix + jnp.concatenate(ends, axis=0)
-    gb_ref[0] = jnp.exp(-bl_ref[0]) * rows[2:4]
+    gd_ref[...] = suffix + jnp.concatenate(ends, axis=0)
+    gb_ref[...] = jnp.exp(-bl_ref[...]) * rows[2:4]
     qf = q.astype(F32)
     kf = k.astype(F32)
     gq_ref[...] = eq - qf * (rq * rq * jnp.sum(qf * eq, axis=1, keepdims=True))
     gk_ref[...] = ek - kf * (rk * rk * jnp.sum(kf * ek, axis=1, keepdims=True))
-
-
-def wide(width):
-    return pl.BlockSpec((TOK, width), lambda i: (0, i))
-
-
-def whole_spec():
-    return pl.BlockSpec((1, 2, TOK), lambda i: (i, 0, 0))
-
-
-def per_head(*shape):
-    return pl.BlockSpec((2,) + shape, lambda i: (i,) + (0,) * len(shape))
-
-
-SAVED = [
-    ((2, TOK, TOK), BF16),
-    ((2, TOK, TOK), BF16),
-    ((TOK, TOK), F32),
-    ((TOK, D), F32),
-    ((2, TOK, D), BF16),
-    ((TOK, D), F32),
-]
-AUX_SPEC = pl.BlockSpec((1, TOK, D), lambda i: (i, 0, 0))
-PARAMS = dict(vmem_limit_bytes=56 * 1024 * 1024)
-
-
-def run_phase1(q, k, v, go, ld, bl):
-    return pl.pallas_call(
-        phase1,
-        grid=(KHEADS,),
-        in_specs=[wide(D), wide(D), wide(2 * D), wide(2 * D), whole_spec(), whole_spec()],
-        out_specs=[per_head(3, D, D)] + [per_head(*s) for s, _ in SAVED] + [AUX_SPEC, per_head(8, D)],
-        out_shape=[jax.ShapeDtypeStruct((HEADS, 3, D, D), F32)]
-        + [jax.ShapeDtypeStruct((HEADS,) + s, t) for s, t in SAVED]
-        + [jax.ShapeDtypeStruct((KHEADS, TOK, D), F32), jax.ShapeDtypeStruct((HEADS, 8, D), F32)],
-        compiler_params=pltpu.CompilerParams(**PARAMS),
-        name="local_transitions",
-    )(q, k, v, go, ld.reshape(KHEADS, 2, TOK), bl.reshape(KHEADS, 2, TOK))
-
-
-def run_phase3(q, k, v, go, bl, sg, saved):
-    *outs, gd, gb = pl.pallas_call(
-        phase3,
-        grid=(KHEADS,),
-        in_specs=[wide(D), wide(D), wide(2 * D), wide(2 * D), whole_spec(), per_head(2, D, D)]
-        + [per_head(*s) for s, _ in SAVED] + [AUX_SPEC, per_head(8, D)],
-        out_specs=[wide(2 * D), wide(D), wide(D), wide(2 * D), whole_spec(), whole_spec()],
-        out_shape=[
-            jax.ShapeDtypeStruct((TOK, HEADS * D), F32),
-            jax.ShapeDtypeStruct((TOK, KHEADS * D), F32),
-            jax.ShapeDtypeStruct((TOK, KHEADS * D), F32),
-            jax.ShapeDtypeStruct((TOK, HEADS * D), F32),
-            jax.ShapeDtypeStruct((KHEADS, 2, TOK), F32),
-            jax.ShapeDtypeStruct((KHEADS, 2, TOK), F32),
-        ],
-        compiler_params=pltpu.CompilerParams(**PARAMS),
-        name="local_gradients",
-    )(q, k, v, go, bl.reshape(KHEADS, 2, TOK), sg, *saved)
-    return (*outs, gd.reshape(HEADS, TOK), gb.reshape(HEADS, TOK))
 
 
 MESH = pl.DeviceIdType.MESH
@@ -310,8 +253,20 @@
     return states, grads[::-1]
 
 
-def scan_kernel(tri_ref, sg_ref, zin, cout, cin, xout, xin, yin, xdo, xdi, cdo, cdi, zdo,
-                own, zs, zr, cs, cr, xs, xr, ys, yr, xds, xdr, cds, cdr, zds, zdr):
+def place(i):
+    own = lax.div(i, 6)
+    r = lax.rem(i, 3)
+    d = (1 - own) * lax.div(3 * r * r + 4 - 5 * r, 2)
+    half = (1 - own) * lax.div(i, 3) + own * (i - 6)
+    return d, half
+
+
+def layer_kernel(q_hbm, k_hbm, v_hbm, go_hbm, ld_ref, bl_ref,
+                 out_hbm, gq_hbm, gk_hbm, gv_hbm, gd_ref, gb_ref,
+                 qb, kb, vb, gob, t_ref, m_ref, gam_ref, u_ref, w_ref, r_ref, aux_ref, end_ref,
+                 tri, zin, cout, cin, xout, xin, yin, xdo, xdi, cdo, cdi, zdo, sgin,
+                 outb, gqb, gkb, gvb,
+                 ins, outs, zs, zr, cs, cr, xs, xr, ys, yr, xds, xdr, cds, cdr, zds, zdr):
     ctx = lax.axis_index("ctx")
     z = lax.axis_index("grp")
     c = lax.rem(ctx, NC)
@@ -338,59 +293,96 @@
     peers += [at(ypeer(d), x, c, z) for d in range(1, NY)]
     for peer in peers:
         pl.semaphore_signal(barrier, inc=1, device_id=peer, device_id_type=MESH)
-    pl.semaphore_wait(barrier, len(peers))
+
+    def up_step(i):
+        d, half = place(i)
+        core = lax.rem(oc + half, NC)
+        return d, half, core, NC * zpeer(d) + core
+
+    def down_step(i):
+        d, half = place(lax.rem(i + 6, 8))
+        core = lax.rem(c + half, NC)
+        return d, half, core, NC * lax.rem(z + NZ - d, NZ) + core
+
+    def loads(kh):
+        one = pl.ds(pl.multiple_of(kh * D, D), D)
+        two = pl.ds(pl.multiple_of(kh * 2 * D, 2 * D), 2 * D)
+        return [
+            pltpu.make_async_copy(q_hbm.at[:, one], qb.at[kh], ins.at[0, kh]),
+            pltpu.make_async_copy(k_hbm.at[:, one], kb.at[kh], ins.at[1, kh]),
+            pltpu.make_async_copy(v_hbm.at[:, two], vb.at[kh], ins.at[2, kh]),
+            pltpu.make_async_copy(go_hbm.at[:, two], gob.at[kh], ins.at[3, kh]),
+        ]
+
+    def stores(kh):
+        one = pl.ds(pl.multiple_of(kh * D, D), D)
+        two = pl.ds(pl.multiple_of(kh * 2 * D, 2 * D), 2 * D)
+        return [
+            pltpu.make_async_copy(outb.at[kh], out_hbm.at[:, two], outs.at[0, kh]),
+            pltpu.make_async_copy(gqb.at[kh], gq_hbm.at[:, one], outs.at[1, kh]),
+            pltpu.make_async_copy(gkb.at[kh], gk_hbm.at[:, one], outs.at[2, kh]),
+            pltpu.make_async_copy(gvb.at[kh], gv_hbm.at[:, two], outs.at[3, kh]),
+        ]
+
+    def load_start(i, _):
+        for copy in loads(up_step(i)[3]):
+            copy.start()
+        return 0
+
+    lax.fori_loop(0, KHEADS, load_start, 0)
 
     def remote(src, dst, send, recv, peer):
         return pltpu.make_async_remote_copy(
             src_ref=src, dst_ref=dst, send_sem=send, recv_sem=recv, device_id=peer, device_id_type=MESH)
 
-    def slot(i):
-        return lax.rem(i + PAIR * oc, SHARE)
-
-    def zcopy(d, i):
+    def zcopy(d, half):
         to = zpeer(d)
-        return remote(tri_ref.at[SHARE * to + slot(i)], zin.at[z, slot(i)], zs.at[d - 1, i], zr.at[d - 1, i],
+        core = lax.rem(oc + half, NC)
+        return remote(tri.at[NC * to + core], zin.at[z, core], zs.at[d - 1, half], zr.at[d - 1, half],
                       at(y, x, c, to))
 
-    mine = pltpu.make_async_copy(tri_ref.at[pl.ds(SHARE * z, SHARE)], zin.at[z], own.at[0])
-    mine.start()
-
-    def zstart(i, _):
-        for d in (2, 1, 3):
-            zcopy(d, i).start()
+    def ccopy():
+        return remote(cout, cin.at[c], cs, cr, at(y, x, oc, z))
+
+    def zjoin(core, half, dst):
+        for d in range(1, NZ):
+            zcopy(d, half).wait_recv()
+        for i in range(PAIR):
+            got = join_all([tuple(zin[m, core, i, p] for p in range(3)) for m in range(NZ)])
+            for p in range(3):
+                dst[i, p] = got[p]
+
+    pl.semaphore_wait(barrier, len(peers))
+
+    def up(i, _):
+        d, half, core, kh = up_step(i)
+        for copy in loads(kh):
+            copy.wait()
+        pair = pl.ds(PAIR * kh, PAIR)
+        phase1(qb.at[kh], kb.at[kh], vb.at[kh], gob.at[kh], ld_ref.at[kh], bl_ref.at[kh], tri.at[kh],
+               t_ref.at[pair], m_ref.at[pair], gam_ref.at[pair], u_ref.at[pair], w_ref.at[pair], r_ref.at[pair],
+               aux_ref.at[kh], end_ref.at[pair])
+
+        @pl.when(i < 6)
+        def _():
+            zcopy(d, half).start()
+
+        @pl.when(i >= 6)
+        def _():
+            zin[z, core] = tri[kh]
+
+        @pl.when(i == 6)
+        def _():
+            zjoin(oc, 0, cout)
+            ccopy().start()
+
         return 0
 
-    lax.fori_loop(0, SHARE, zstart, 0)
-    mine.wait()
-
-    def ccopy(i):
-        return remote(cout.at[i], cin.at[c, i], cs.at[i], cr.at[i], at(y, x, oc, z))
-
-    def zjoin(i):
-        for d in range(1, NZ):
-            zcopy(d, i).wait_recv()
-        h = slot(i)
-        return join_all([tuple(zin[m, h, p] for p in range(3)) for m in range(NZ)])
-
-    def zaway(i, _):
-        got = zjoin(i)
-        for p in range(3):
-            cout[i, p] = got[p]
-        ccopy(i).start()
-        return 0
-
-    lax.fori_loop(0, PAIR, zaway, 0)
-
-    def zhere(i, _):
-        got = zjoin(i + PAIR)
-        for p in range(3):
-            cin[c, i, p] = got[p]
-        return 0
-
-    lax.fori_loop(0, PAIR, zhere, 0)
-
+    lax.fori_loop(0, KHEADS, up, 0)
+    zjoin(c, 1, cin.at[c])
+
+    ccopy().wait_recv()
     for i in range(PAIR):
-        ccopy(i).wait_recv()
         a, b, g = join_all([tuple(cin[m, i, p] for p in range(3)) for m in range(NC)])
         for half in range(2):
             to = 2 * i + half
@@ -455,76 +447,116 @@
     cdcopy.start()
     cdi[c] = cdo[c]
 
-    def zdcopy(d, h):
+    def zdcopy(d, half):
         to = zpeer(d)
-        return remote(zdo.at[to, h], sg_ref.at[SHARE * z + h], zds.at[d - 1, h], zdr.at[d - 1, h], at(y, x, c, to))
-
-    def zdown(core):
-        def body(i, _):
-            h = PAIR * core + i
-            parts = [tuple(zin[m, h, p] for p in range(3)) for m in range(NZ)]
+        core = lax.rem(c + half, NC)
+        return remote(zdo.at[to, core], sgin.at[z, core], zds.at[d - 1, half], zdr.at[d - 1, half], at(y, x, c, to))
+
+    def zdown(half, _):
+        core = lax.rem(c + half, NC)
+
+        @pl.when(half == 1)
+        def _():
+            cdcopy.wait_recv()
+
+        for i in range(PAIR):
+            parts = [tuple(zin[m, core, i, p] for p in range(3)) for m in range(NZ)]
             states, grads = chain(parts, cdi[core, i, 0], cdi[core, i, 1])
             for m in range(NZ):
-                zdo[m, h, 0] = states[m]
-                zdo[m, h, 1] = grads[m]
-            for d in (2, 1, 3):
-                zdcopy(d, h).start()
-            return 0
-
-        lax.fori_loop(0, PAIR, body, 0)
-
-    zdown(c)
-    cdcopy.wait_recv()
-    zdown(oc)
-    mine = pltpu.make_async_copy(zdo.at[z], sg_ref.at[pl.ds(SHARE * z, SHARE)], own.at[1])
-    mine.start()
-
-    def zwait(i, _):
+                zdo[m, core, i, 0] = states[m]
+                zdo[m, core, i, 1] = grads[m]
+        for d in (2, 1, 3):
+            zdcopy(d, half).start()
+        sgin[z, core] = zdo[z, core]
+        return 0
+
+    lax.fori_loop(0, NC, zdown, 0)
+
+    def down(i, _):
+        d, half, core, kh = down_step(i)
+
+        @pl.when(i >= 2)
+        def _():
+            zdcopy(d, half).wait_recv()
+
+        pair = pl.ds(PAIR * kh, PAIR)
+        phase3(qb.at[kh], kb.at[kh], vb.at[kh], gob.at[kh], bl_ref.at[kh], sgin.at[lax.div(kh, NC), core],
+               t_ref.at[pair], m_ref.at[pair], gam_ref.at[pair], u_ref.at[pair], w_ref.at[pair], r_ref.at[pair],
+               aux_ref.at[kh], end_ref.at[pair],
+               outb.at[kh], gqb.at[kh], gkb.at[kh], gvb.at[kh], gd_ref.at[kh], gb_ref.at[kh])
+        for copy in stores(kh):
+            copy.start()
+        return 0
+
+    lax.fori_loop(0, KHEADS, down, 0)
+
+    for half in range(2):
         for d in range(1, NZ):
-            zcopy(d, i).wait_send()
-            zdcopy(d, i).wait()
-        return 0
-
-    lax.fori_loop(0, SHARE, zwait, 0)
-    for i in range(PAIR):
-        ccopy(i).wait_send()
+            zcopy(d, half).wait_send()
+            zdcopy(d, half).wait_send()
+    ccopy().wait_send()
     for d in range(1, NX):
         xcopy(d).wait_send()
         xdcopy(d).wait_send()
     for d in range(1, NY):
         ycopy(d).wait_send()
     cdcopy.wait_send()
-    mine.wait()
-
-
-def run_scan(tri):
+
+    def store_wait(kh, _):
+        for copy in stores(kh):
+            copy.wait()
+        return 0
+
+    lax.fori_loop(0, KHEADS, store_wait, 0)
+
+
+def run_layer(q, k, v, go, ld, bl):
     dma = pltpu.SemaphoreType.DMA
-    vm = lambda *shape: pltpu.VMEM(shape, F32)
-    return pl.pallas_call(
-        scan_kernel,
-        in_specs=[pl.BlockSpec(memory_space=pl.ANY)],
-        out_specs=pl.BlockSpec(memory_space=pl.ANY),
-        out_shape=jax.ShapeDtypeStruct((HEADS, 2, D, D), F32),
+
+    def vm(*shape, dtype=F32):
+        return pltpu.VMEM(shape, dtype)
+
+    hbm = pl.BlockSpec(memory_space=pl.ANY)
+    vmem = pl.BlockSpec(memory_space=pltpu.VMEM)
+    *outs, gd, gb = pl.pallas_call(
+        layer_kernel,
+        in_specs=[hbm] * 4 + [vmem] * 2,
+        out_specs=[hbm] * 4 + [vmem] * 2,
+        out_shape=[
+            jax.ShapeDtypeStruct((TOK, HEADS * D), F32),
+            jax.ShapeDtypeStruct((TOK, KHEADS * D), F32),
+            jax.ShapeDtypeStruct((TOK, KHEADS * D), F32),
+            jax.ShapeDtypeStruct((TOK, HEADS * D), F32),
+            jax.ShapeDtypeStruct((KHEADS, 2, TOK), F32),
+            jax.ShapeDtypeStruct((KHEADS, 2, TOK), F32),
+        ],
         scratch_shapes=[
-            vm(NZ, SHARE, 3, D, D), vm(PAIR, 3, D, D), vm(NC, PAIR, 3, D, D),
+            vm(KHEADS, TOK, D, dtype=BF16), vm(KHEADS, TOK, D, dtype=BF16),
+            vm(KHEADS, TOK, 2 * D, dtype=BF16), vm(KHEADS, TOK, 2 * D, dtype=BF16),
+            vm(HEADS, 2, TOK, TOK, dtype=BF16), vm(HEADS, 2, TOK, TOK, dtype=BF16), vm(HEADS, TOK, TOK),
+            vm(HEADS, TOK, D), vm(HEADS, 2, TOK, D, dtype=BF16), vm(HEADS, TOK, D),
+            vm(KHEADS, TOK, D), vm(HEADS, 8, D),
+            vm(KHEADS, PAIR, 3, D, D), vm(NZ, NC, PAIR, 3, D, D),
+            vm(PAIR, 3, D, D), vm(NC, PAIR, 3, D, D),
             vm(NX, 2 * D, D), vm(NX, 2 * D, D), vm(NY, 2 * D, D),
             vm(NX, D, D), vm(NX, D, D), vm(NC, PAIR, 2, D, D), vm(NC, PAIR, 2, D, D),
-            vm(NZ, SHARE, 2, D, D),
-            dma((2,)),
-            dma((NZ - 1, SHARE)), dma((NZ - 1, SHARE)), dma((PAIR,)), dma((PAIR,)),
+            vm(NZ, NC, PAIR, 2, D, D), vm(NZ, NC, PAIR, 2, D, D),
+            vm(KHEADS, TOK, 2 * D), vm(KHEADS, TOK, D), vm(KHEADS, TOK, D), vm(KHEADS, TOK, 2 * D),
+            dma((4, KHEADS)), dma((4, KHEADS)),
+            dma((NZ - 1, 2)), dma((NZ - 1, 2)), dma, dma,
             dma((NX - 1,)), dma((NX - 1,)), dma((NY - 1,)), dma((NY - 1,)),
             dma((NX - 1,)), dma((NX - 1,)), dma, dma,
-            dma((NZ - 1, SHARE)), dma((NZ - 1, SHARE)),
+            dma((NZ - 1, 2)), dma((NZ - 1, 2)),
         ],
-        compiler_params=pltpu.CompilerParams(collective_id=0, has_side_effects=True, **PARAMS),
-        name="device_scan",
-    )(tri)
+        compiler_params=pltpu.CompilerParams(
+            collective_id=0, has_side_effects=True, vmem_limit_bytes=VMEM_LIMIT),
+        name="delta_layer",
+    )(q, k, v, go, ld.reshape(KHEADS, 2, TOK), bl.reshape(KHEADS, 2, TOK))
+    return (*outs, gd.reshape(HEADS, TOK), gb.reshape(HEADS, TOK))
 
 
 def on_device(query_rows, key_rows, value_rows, log_decay, beta_logit, grad_out):
-    tri, *saved = run_phase1(query_rows, key_rows, value_rows, grad_out, log_decay, beta_logit)
-    sg = run_scan(tri)
-    return run_phase3(query_rows, key_rows, value_rows, grad_out, beta_logit, sg, saved)
+    return run_layer(query_rows, key_rows, value_rows, grad_out, log_decay, beta_logit)
 
 
 def solution(mesh):

time: 160 us -> 119 us (0.74)
  Pallas kernels: 153 us -> 106 us
  local copies, waits for them, and re-layouts: 5.34 us -> 12 us
    pallas_call x3 -> x1, Pallas kernels: 153 us -> 106 us  [run_layer(): pl.pallas_call(layer_kernel, in_specs=[hbm] * 4 + [vmem] * 2, out_specs=[...]
    unnamed x0 -> x10, local copies, waits for them, and re-layouts: none -> 6.62 us
where the time goes in v2:
time: 119 us; the launch traced here: 118 us
  Pallas kernels  106 us (89%)
  local copies, waits for them, and re-layouts  12 us (10%)
    pallas_call x1, Pallas kernels, run_layer(): pl.pallas_call(layer_kernel, in_specs=[hbm] * 4 + [vmem] * 2, out_specs=[...  106 us
    unnamed x10, local copies, waits for them, and re-layouts  6.62 us
    reshape x2, local copies, waits for them, and re-layouts, run_layer(): return (*outs, gd.reshape(HEADS, TOK), gb.reshape(HEADS, TOK))  2.67 us

profile of v2, /device:TPU:0, one launch (start us, length us, event | category | flops | bytes accessed | tf_op | source)
XLA Modules:
  0.0 118.3 jit_solution(4977691237168313806)
XLA Ops:
  0.6 1.3 %reshape.24.ld_ref = f32[8,2,256]{2,1,0:T(2,128)} reshape(f32[16,256]{1,0:T(8,128)} %param.9) | data formatting | bytes 32768 | tf_op jit(solution)/shard_map/reshape | solution.py:554
  2.0 1.3 %reshape.25.bl_ref = f32[8,2,256]{2,1,0:T(2,128)} reshape(f32[16,256]{1,0:T(8,128)} %param.10) | data formatting | bytes 32768 | tf_op jit(solution)/shard_map/reshape | solution.py:554
  3.3 105.7 %delta_layer.1 = (f32[256,2048]{1,0:T(8,128)}, f32[256,1024]{1,0:T(8,128)}, f32[256,1024]{1,0:T(8,128)}, f32[256,2048]{1,0:T(8,128)}, f32[8,2,256]{2,1,0:T(2,128)}, /*index=5*/f32[8,2,256]{2,1,0:T(2,128)}) custom-call(bf16[256,1024]{1,0:T(8,128)(2,1)} %q_hbm.1, bf16[256,1024]{1,0:T(8,128)(2,1)} %k_hbm.1, bf16[256,2048]{1,0:T(8,128)(2,1)} %v_hbm.1, ...), custom_call_target="tpu_custom_call" | custom-call | tf_op jit(solution)/shard_map/delta_layer/pallas_call | solution.py:521
  109.0 1.3 %reshape.26 = f32[16,256]{1,0:T(8,128)} reshape(f32[8,2,256]{2,1,0:T(2,128)} %get-tuple-element.16) | data formatting | bytes 32768 | tf_op jit(solution)/shard_map/reshape | solution.py:555
  110.3 1.3 %reshape.27 = f32[16,256]{1,0:T(8,128)} reshape(f32[8,2,256]{2,1,0:T(2,128)} %get-tuple-element.17) | data formatting | bytes 32768 | tf_op jit(solution)/shard_map/reshape | solution.py:555
  111.7 0.0 copy-start.2
  111.7 0.0 copy-start.1
  111.7 3.3 %copy.16 = f32[256,2048]{1,0:T(8,128)} copy(f32[256,2048]{1,0:T(8,128)} %get-tuple-element.24) | data formatting | bytes 4194304
  115.0 0.0 copy-done.2
  115.0 0.0 copy-start
  115.0 1.0 copy.17
  115.9 0.0 copy-done.1
  115.9 1.0 copy.18
  116.9 0.1 copy-done
  117.0 1.3 %copy.19 = f32[256,2048]{1,0:T(8,128)} copy(f32[256,2048]{1,0:T(8,128)S(1)} %copy-done) | data formatting | bytes 4194304
Async XLA Ops:
  111.7 3.3 %copy-start.2 = (f32[256,1024]{1,0:T(8,128)S(1)}, f32[256,1024]{1,0:T(8,128)}, u32[]{:S(2)}) copy-start(f32[256,1024]{1,0:T(8,128)} %get-tuple-element.25) | copy-start | bytes 3145732
  111.7 4.3 %copy-start.1 = (f32[256,1024]{1,0:T(8,128)S(1)}, f32[256,1024]{1,0:T(8,128)}, u32[]{:S(2)}) copy-start(f32[256,1024]{1,0:T(8,128)} %get-tuple-element.26) | copy-start | bytes 3145732
  115.0 2.0 %copy-start = (f32[256,2048]{1,0:T(8,128)S(1)}, f32[256,2048]{1,0:T(8,128)}, u32[]{:S(2)}) copy-start(f32[256,2048]{1,0:T(8,128)} %get-tuple-element.27) | copy-start | bytes 6291460

commit v3 on v2

v3 whole, which is shorter than its diff:
```python
import jax
import jax.numpy as jnp
from jax import lax
from jax.experimental import pallas as pl
from jax.experimental.pallas import tpu as pltpu
from jax.sharding import PartitionSpec as P

F32 = jnp.float32
BF16 = jnp.bfloat16
TOK = 256
D = 128
HEADS = 16
KHEADS = 8


def dg(a, b, ca, cb):
    return lax.dot_general(a, b, (((ca,), (cb,)), ((), ())), preferred_element_type=F32)


def split(x):
    hi = x.astype(BF16)
    return hi, (x - hi.astype(F32)).astype(BF16)


def halves(both):
    n = both.shape[1] // 2
    return both[:, :n] + both[:, n:]


def dot4(a, b, ca, cb):
    wide = jnp.concatenate(b, axis=1 - cb)
    return halves(dg(jnp.concatenate(a, axis=ca), jnp.concatenate([wide, wide], axis=cb), ca, cb))


def dot2r(a, b, ca, cb):
    return halves(dg(a, jnp.concatenate(b, axis=1 - cb), ca, cb))


def dot2l(a, b, ca, cb):
    return dg(a[0], b, ca, cb) + dg(a[1], b, ca, cb)


def dot3(a, b, ca, cb):
    return dot2r(a[0], b, ca, cb) + dg(a[1], b[0], ca, cb)


def iota(shape, dim):
    return lax.broadcasted_iota(jnp.int32, shape, dim)


def cumulate(rows, tri):
    hi = rows.astype(BF16)
    rest = rows - hi.astype(F32)
    mid = rest.astype(BF16)
    low = (rest - mid.astype(F32)).astype(BF16)
    parts = jnp.concatenate([hi.astype(F32), mid.astype(F32), low.astype(F32), jnp.zeros((2, TOK), F32)], axis=0)
    got = dg(parts.astype(BF16), tri, 1, 0)
    return got[0:2] + (got[2:4] + got[4:6])


def invert(systems):
    n = len(systems)
    lane = iota((16, D), 1)
    row = iota((16, D), 0)
    block = lane // 16
    packed = []
    for mat in systems:
        got = jnp.where(block == 0, mat[0:16], 0.0)
        for i in range(1, 8):
            got = jnp.where(block == i, mat[16 * i : 16 * i + 16], got)
        packed.append(got)
    inv = [jnp.where(lane % 16 == row, 1.0, 0.0).astype(F32) for _ in range(n)]
    for m in range(15):
        index = block * 16 + m
        for c in range(n):
            column = jnp.take_along_axis(packed[c], index, axis=1, mode="promise_in_bounds")
            inv[c] = inv[c] - column * inv[c][m : m + 1, :]
    wide_r = iota((D, D), 0)
    wide_c = iota((D, D), 1)
    full = [
        jnp.concatenate([jnp.where(block == i, inv[c], 0.0) for i in range(8)], axis=0)
        for c in range(n)
    ]
    for b in (16, 32, 64):
        mask = (wide_r // (2 * b) == wide_c // (2 * b)) & (wide_r // b % 2 == 1) & (wide_c // b % 2 == 0)
        sides = [split(jnp.where(mask, systems[c], 0.0)) for c in range(n)]
        ts = [split(full[c]) for c in range(n)]
        inner = [split(dot4(sides[c], ts[c], 1, 0)) for c in range(n)]
        full = [full[c] - dot4(ts[c], inner[c], 1, 0) for c in range(n)]
    return full


def rows_to_cols(rows8):
    return jnp.concatenate([rows8] * 16, axis=0).T


def cols_to_rows(cols):
    lane = iota((TOK, D), 1)
    got = jnp.zeros((TOK, D), F32)
    for i, col in enumerate(cols):
        got = jnp.where(lane == i, col, got)
    return got.T


VMEM_LIMIT = 60 * 1024 * 1024


def phase1(q_ref, k_ref, v_ref, go_ref, ld_ref, bl_ref,
           tri_ref, t_ref, m_ref, gam_ref, u_ref, w_ref, r_ref, aux_ref, end_ref):
    both = range(2)
    t_i = iota((TOK, TOK), 0)
    s_i = iota((TOK, TOK), 1)
    upper = jnp.where(t_i <= s_i, 1.0, 0.0).astype(BF16)
    within = t_i >= s_i
    q = [q_ref[:, j * D : (j + 1) * D] for j in both]
    k = [k_ref[:, j * D : (j + 1) * D] for j in both]
    kk = [dg(k[j], k[j], 1, 1) for j in both]
    qk = [dg(q[j], k[j], 1, 1) for j in both]
    run = cumulate(ld_ref[...], upper)
    beta_rows = 1.0 / (1.0 + jnp.exp(-bl_ref[...]))
    last = run[:, TOK - 1 : TOK]
    grown = jnp.exp(run)
    cols = rows_to_cols(jnp.concatenate([run, beta_rows, grown, jnp.exp(last - run)], axis=0))
    lane = iota((TOK, D), 1)
    kf = [part.astype(F32) for part in k]
    for j in both:
        for i, part in ((8, q[j].astype(F32)), (10, kf[j])):
            norm = lax.rsqrt(jnp.sum(part * part, axis=1, keepdims=True) + 1e-6)
            cols = jnp.where(lane == i + j, norm, cols)
    aux_ref[...] = cols
    norm_rows = cols.T
    rq = [cols[:, 8 + j : 9 + j] for j in both]
    rk = [cols[:, 10 + j : 11 + j] for j in both]
    g = [cols[:, 4 + j : 5 + j] for j in both]
    frk = [cols[:, 6 + j : 7 + j] * rk[j] for j in both]
    gam = [jnp.exp(jnp.where(within, cols[:, j : j + 1] - run[j : j + 1], -1e30)) * norm_rows[10 + j : 11 + j]
           for j in both]
    systems = [jnp.where(t_i > s_i, kk[j] * gam[j] * (cols[:, 2 + j : 3 + j] * rk[j]), 0.0) for j in both]
    blocks = []
    for j in both:
        blocks += [systems[j][:D, :D], systems[j][D:, D:]]
    mix = [split(qk[j] * gam[j] * rq[j]) for j in both]
    go_t = [go_ref[j].T for j in both]
    r_t = [dg(go_t[j], mix[j][0], 1, 0) + dg(go_t[j], mix[j][1], 1, 0) for j in both]
    for j in both:
        gam_ref[j] = gam[j]
        m_ref[j, 0] = mix[j][0]
        m_ref[j, 1] = mix[j][1]
        r_ref[j] = r_t[j]
    inv = [split(block) for block in invert(blocks)]
    inner = [split(dot4(split(systems[j][D:, :D]), inv[2 * j], 1, 0)) for j in both]
    t21 = [split(-dot4(inv[2 * j + 1], inner[j], 1, 0)) for j in both]
    tb = []
    for j in both:
        whole = []
        for i in range(2):
            t11, t22 = inv[2 * j][i], inv[2 * j + 1][i]
            whole.append(jnp.concatenate(
                [jnp.concatenate([t11, jnp.zeros((D, D), BF16)], axis=1),
                 jnp.concatenate([t21[j][i], t22], axis=1)], axis=0))
        tb.append(split((whole[0].astype(F32) + whole[1].astype(F32)) * beta_rows[j : j + 1]))
    ks = [split(kf[j] * (g[j] * rk[j])) for j in both]
    uw = [dot2l(tb[j], jnp.concatenate([v_ref[j], ks[j][0]], axis=1), 1, 0) for j in both]
    w = [uw[j][:, D:] + dg(tb[j][0], ks[j][1], 1, 0) for j in both]
    ws = [split(w[j]) for j in both]
    ends = [jnp.exp(last[j : j + 1]) for j in both]
    ab = [dot2r(k[j].T, split(jnp.concatenate([w[j] * frk[j], uw[j][:, :D] * frk[j]], axis=1)), 1, 0) for j in both]
    go_g = [split(go_t[j].astype(F32) * (grown[j : j + 1] * norm_rows[8 + j : 9 + j])) for j in both]
    offset = [dot2l(go_g[j], q[j], 1, 0) for j in both]
    offset = [offset[j] - dot3(split(r_t[j]), ws[j], 1, 0) for j in both]
    eye = jnp.where(iota((D, D), 0) == iota((D, D), 1), 1.0, 0.0)
    for j in both:
        tri_ref[j, 0] = eye * ends[j] - ab[j][:, :D]
        tri_ref[j, 1] = ab[j][:, D:].T
        tri_ref[j, 2] = offset[j]
        t_ref[j, 0] = tb[j][0]
        t_ref[j, 1] = tb[j][1]
        u_ref[j] = uw[j][:, :D]
        w_ref[j, 0] = ws[j][0]
        w_ref[j, 1] = ws[j][1]
        end_ref[j] = jnp.broadcast_to(ends[j], (8, D))


def phase3(part, q_ref, k_ref, v_ref, go_ref, bl_ref, sg_ref, t_ref, m_ref, gam_ref, u_ref, w_ref, r_ref, aux_ref,
           end_ref, out_ref, gq_ref, gk_ref, gv_ref, gd_ref, gb_ref):
    both = range(2)
    aux = aux_ref[...]
    aux_rows = aux.T
    frk_rows = aux_rows[6:8] * aux_rows[10:12]
    t_i = iota((TOK, TOK), 0)
    s_i = iota((TOK, TOK), 1)
    strict = t_i > s_i
    lower = jnp.where(t_i >= s_i, 1.0, 0.0).astype(BF16)
    q = [q_ref[:, j * D : (j + 1) * D] for j in both]
    k = [k_ref[:, j * D : (j + 1) * D] for j in both]
    v = [v_ref[j] for j in both]
    go = [go_ref[j] for j in both]
    rq = [aux[:, 8 + j : 9 + j] for j in both]
    rk = [aux[:, 10 + j : 11 + j] for j in both]
    g = [aux[:, 4 + j : 5 + j] for j in both]
    frk = [aux[:, 6 + j : 7 + j] * rk[j] for j in both]
    ss = [split(sg_ref[j, 0]) for j in both]
    gs = [split(sg_ref[j, 1]) for j in both]
    xw = [dot4((w_ref[j, 0], w_ref[j, 1]), ss[j], 1, 1) for j in both]
    kg = [dg(jnp.concatenate(gs[j], axis=0), k[j], 1, 1) for j in both]
    qs = [dot2r(q[j], ss[j], 1, 1) for j in both]
    gos = [dot2r(go[j], ss[j], 1, 0) for j in both]
    x = [u_ref[j] - xw[j] for j in both]
    xs = [split(x[j]) for j in both]
    dx_t = [split(r_ref[j] + (kg[j][:D] + kg[j][D:]) * frk_rows[j : j + 1]) for j in both]
    y_t = [dg(dx_t[j][0], t_ref[j, 0], 1, 0) + (dg(dx_t[j][0], t_ref[j, 1], 1, 0) + dg(dx_t[j][1], t_ref[j, 0], 1, 0))
           for j in both]
    gx = [dg(jnp.concatenate([go[j], go[j]], axis=1), jnp.concatenate(xs[j], axis=1), 1, 1) for j in both]
    y = [y_t[j].T for j in both]
    ys = [split(y[j]) for j in both]
    for j in both:
        gv_ref[j] = y[j]
    mx = [dot3((m_ref[j, 0], m_ref[j, 1]), xs[j], 1, 0) for j in both]
    n = [split(gx[j] * gam_ref[j] * rq[j]) for j in both]
    yx = [dg(jnp.concatenate(ys[j], axis=1), jnp.concatenate([xs[j][0], xs[j][0]], axis=1), 1, 1)
          + dg(ys[j][0], xs[j][1], 1, 1) for j in both]
    out = [qs[j] * (g[j] * rq[j]) + mx[j] for j in both]
    for j in both:
        out_ref[j] = out[j]
    k_t = [k[j].T for j in both]
    q_t = [q[j].T for j in both]
    xk = [dot2r(k_t[j], split(x[j] * frk[j]), 1, 0) for j in both]
    ends = [jnp.sum(sg_ref[j, 1] * (sg_ref[j, 0] * end_ref[j][0:1] + xk[j].T), keepdims=True) for j in both]
    turned = [dg(q_t[j], n[j][0], 1, 0) + dg(q_t[j], n[j][1], 1, 0) for j in both]
    eq = [dot2l(n[j], k[j], 1, 0) for j in both]
    p = [split(jnp.where(strict, yx[j] * gam_ref[j] * (-rk[j]), 0.0)) for j in both]
    turned = [turned[j] + (dg(k_t[j], p[j][0], 1, 0) + dg(k_t[j], p[j][1], 1, 0)) for j in both]
    ek = [dot2l(p[j], k[j], 1, 0) for j in both]
    xg = [dot4(xs[j], gs[j], 1, 0) for j in both]
    sy = [dot4(ys[j], ss[j], 1, 0) for j in both]
    eq = [eq[j] + gos[j] * (g[j] * rq[j]) for j in both]
    ek = [ek[j] + turned[j].T + (xg[j] * frk[j] - sy[j] * (g[j] * rk[j])) for j in both]
    dots = [jnp.sum(go[j].astype(F32) * out[j] - v[j].astype(F32) * y[j], axis=1, keepdims=True) for j in both]
    dots += [jnp.sum(y[j] * x[j], axis=1, keepdims=True) for j in both]

    @pl.when(part == 0)
    def _():
        for j in both:
            gq_ref[:, j * D : (j + 1) * D] = eq[j]
            gk_ref[:, j * D : (j + 1) * D] = ek[j]

    @pl.when(part == 1)
    def _():
        for j in both:
            cols = slice(j * D, (j + 1) * D)
            for raw, ref, row, norm in ((q[j], gq_ref, eq[j], rq[j]), (k[j], gk_ref, ek[j], rk[j])):
                row = row + ref[:, cols]
                raw = raw.astype(F32)
                ref[:, cols] = row - raw * (norm * norm * jnp.sum(raw * row, axis=1, keepdims=True))

    rows = cols_to_rows(dots)
    suffix = cumulate(rows[0:2], lower)
    gd_ref[...] = suffix + jnp.concatenate(ends, axis=0)
    gb_ref[...] = jnp.exp(-bl_ref[...]) * rows[2:4]


MESH = pl.DeviceIdType.MESH
NZ, NC, NX, NY = 4, 2, 4, 4
SHARE = HEADS // NZ
PARTS = 2
QUARTER = D // NX


def join(early, late):
    ae, be, ce = early
    al, bl, cl = late
    als = split(al)
    cls = split(cl)
    left = (jnp.concatenate([als[0], cls[0]], axis=0), jnp.concatenate([als[1], cls[1]], axis=0))
    both = dot4(left, split(ae), 1, 0)
    return both[:D], dot4(split(be), als, 1, 1) + bl, both[D:] + ce


def join_all(parts):
    while len(parts) > 1:
        parts = [join(parts[i], parts[i + 1]) for i in range(0, len(parts), 2)]
    return parts[0]


def chain(parts, state, grad):
    split_a = [split(p[0]) for p in parts]
    states = [state]
    for i in range(len(parts) - 1):
        states.append(dot4(split(states[-1]), split_a[i], 1, 1) + parts[i][1])
    grads = [grad]
    for i in range(len(parts) - 1, 0, -1):
        grads.append(dot4(split(grads[-1]), split_a[i], 1, 0) + parts[i][2])
    return states, grads[::-1]


def place(i):
    r = lax.rem(i, NZ)
    return lax.rem(lax.div(3 * r * r + 4 - 5 * r, 2), NZ), lax.div(i, NZ)


def layer_kernel(q_hbm, k_hbm, v_hbm, go_hbm, ld_ref, bl_ref,
                 out_hbm, gq_hbm, gk_hbm, gv_hbm, gd_ref, gb_ref,
                 qb, kb, vb, gob, ldp, blp, gdp, gbp, t_ref, m_ref, gam_ref, u_ref, w_ref, r_ref, aux_ref, end_ref,
                 tri, zin, cout, cin, xout, xin, yin, xdo, xdi, cdo, cdi, zdo, sgin,
                 outb, gqb, gkb, gvb,
                 ins, outs, zs, zr, cs, cr, xs, xr, ys, yr, xds, xdr, cds, cdr, zds, zdr):
    ctx = lax.axis_index("ctx")
    z = lax.axis_index("grp")
    c = lax.rem(ctx, NC)
    x = lax.rem(lax.div(ctx, NC), NX)
    y = lax.div(ctx, NC * NX)
    oc = 1 - c

    def at(yy, xx, cc, zz):
        return ((yy * NX + xx) * NC + cc, zz)

    def zpeer(d):
        return lax.rem(z + d, NZ)

    def xpeer(d):
        return lax.rem(x + d, NX)

    def ypeer(d):
        return lax.rem(y + d, NY)

    barrier = pltpu.get_barrier_semaphore()
    peers = [at(y, x, c, zpeer(d)) for d in range(1, NZ)]
    peers += [at(y, x, oc, z)]
    peers += [at(y, xpeer(d), c, z) for d in range(1, NX)]
    peers += [at(ypeer(d), x, c, z) for d in range(1, NY)]
    for peer in peers:
        pl.semaphore_signal(barrier, inc=1, device_id=peer, device_id_type=MESH)

    def lanes(head, width):
        return pl.ds(pl.multiple_of(head * width, width), width)

    def rows_of(zz):
        both = lanes(zz, 2 * D)
        return [pltpu.make_async_copy(q_hbm.at[:, both], qb.at[zz], ins.at[0, zz]),
                pltpu.make_async_copy(k_hbm.at[:, both], kb.at[zz], ins.at[1, zz])]

    def values_of(zz, part):
        copies = []
        for j in range(2):
            one = lanes(SHARE * zz + 2 * j + part, D)
            slot = 2 * zz + part
            copies.append(pltpu.make_async_copy(v_hbm.at[:, one], vb.at[slot, j], ins.at[2 + j, slot]))
            copies.append(pltpu.make_async_copy(go_hbm.at[:, one], gob.at[slot, j], ins.at[4 + j, slot]))
        return copies

    def outputs_of(zz, part):
        copies = []
        for j in range(2):
            one = lanes(SHARE * zz + 2 * j + part, D)
            slot = 2 * zz + part
            copies.append(pltpu.make_async_copy(outb.at[slot, j], out_hbm.at[:, one], outs.at[2 + j, slot]))
            copies.append(pltpu.make_async_copy(gvb.at[slot, j], gv_hbm.at[:, one], outs.at[4 + j, slot]))
        return copies

    def grads_of(zz):
        both = lanes(zz, 2 * D)
        return [pltpu.make_async_copy(gqb.at[zz], gq_hbm.at[:, both], outs.at[0, zz]),
                pltpu.make_async_copy(gkb.at[zz], gk_hbm.at[:, both], outs.at[1, zz])]

    def load_start(i, _):
        d, part = place(i)
        zz = zpeer(d)

        @pl.when(part == 0)
        def _():
            for copy in rows_of(zz):
                copy.start()

        for copy in values_of(zz, part):
            copy.start()
        return 0

    lax.fori_loop(0, NZ * PARTS, load_start, 0)
    for zz in range(NZ):
        for part in range(PARTS):
            for j in range(2):
                h = SHARE * zz + 2 * j + part
                ldp[2 * zz + part, j : j + 1] = ld_ref[h : h + 1]
                blp[2 * zz + part, j : j + 1] = bl_ref[h : h + 1]

    def remote(src, dst, send, recv, peer):
        return pltpu.make_async_remote_copy(
            src_ref=src, dst_ref=dst, send_sem=send, recv_sem=recv, device_id=peer, device_id_type=MESH)

    def zcopy(d, part):
        to = zpeer(d)
        return remote(tri.at[2 * to + part], zin.at[part, z], zs.at[d - 1, part], zr.at[d - 1, part], at(y, x, c, to))

    def ccopy(part):
        return remote(cout.at[part], cin.at[part, c], cs.at[part], cr.at[part], at(y, x, oc, z))

    def xcopy(d, part):
        return remote(xout.at[part, xpeer(d)], xin.at[part, x], xs.at[d - 1, part], xr.at[d - 1, part],
                      at(y, xpeer(d), c, z))

    def ycopy(d, part):
        return remote(yin.at[part, y], yin.at[part, y], ys.at[d - 1, part], yr.at[d - 1, part],
                      at(ypeer(d), x, c, z))

    def xdcopy(d, part):
        return remote(xdo.at[part, xpeer(d)], xdi.at[part, x], xds.at[d - 1, part], xdr.at[d - 1, part],
                      at(y, xpeer(d), c, z))

    def cdcopy(part):
        return remote(cdo.at[part, oc], cdi.at[part], cds.at[part], cdr.at[part], at(y, x, oc, z))

    def zdcopy(d, part, half):
        to = zpeer(d)
        core = lax.rem(c + half, NC)
        pair = NC * part + half
        return remote(zdo.at[part, to, core], sgin.at[part, z, core], zds.at[d - 1, pair], zdr.at[d - 1, pair],
                      at(y, x, c, to))

    def triple(ref):
        return ref[0], ref[1], ref[2]

    def packed(ref):
        return ref[0:D], ref[D : D + QUARTER], ref[D + QUARTER : D + 2 * QUARTER]

    def join_z(part):
        zin[part, z] = tri[2 * z + part]
        for d in range(1, NZ):
            zcopy(d, part).wait_recv()
        got = join_all([triple(zin.at[part, m, oc]) for m in range(NZ)])
        for i in range(3):
            cout[part, i] = got[i]
        ccopy(part).start()
        got = join_all([triple(zin.at[part, m, c]) for m in range(NZ)])
        for i in range(3):
            cin[part, c, i] = got[i]

    def join_core(part):
        ccopy(part).wait_recv()
        a, b, g = join_all([triple(cin.at[part, m]) for m in range(NC)])
        for to in range(NX):
            rows = slice(to * QUARTER, (to + 1) * QUARTER)
            xout[part, to, 0:D] = a
            xout[part, to, D : D + QUARTER] = b[rows]
            xout[part, to, D + QUARTER : D + 2 * QUARTER] = g[rows]
        for d in (2, 1, 3):
            xcopy(d, part).start()
        xin[part, x] = xout[part, x]

    def join_x(part):
        for d in range(1, NX):
            xcopy(d, part).wait_recv()
        row = join_all([packed(xin.at[part, m]) for m in range(NX)])
        yin[part, y, 0:D] = row[0]
        yin[part, y, D : D + QUARTER] = row[1]
        yin[part, y, D + QUARTER : D + 2 * QUARTER] = row[2]
        for d in (2, 1, 3):
            ycopy(d, part).start()

    def down_x(part):
        for d in range(1, NY):
            ycopy(d, part).wait_recv()
        zero = jnp.zeros((QUARTER, D), F32)
        states, grads = chain([packed(yin.at[part, m]) for m in range(NY)], zero, zero)
        state, grad = states[0], grads[0]
        for m in range(1, NY):
            state = jnp.where(y == m, states[m], state)
            grad = jnp.where(y == m, grads[m], grad)
        states, grads = chain([packed(xin.at[part, m]) for m in range(NX)], state, grad)
        for m in range(NX):
            xdo[part, m, 0:QUARTER] = states[m]
            xdo[part, m, QUARTER : 2 * QUARTER] = grads[m]
        for d in (2, 1, 3):
            xdcopy(d, part).start()
        xdi[part, x] = xdo[part, x]

    def down_core(part):
        for d in range(1, NX):
            xdcopy(d, part).wait_recv()
        state = jnp.concatenate([xdi[part, m, 0:QUARTER] for m in range(NX)], axis=0)
        grad = jnp.concatenate([xdi[part, m, QUARTER : 2 * QUARTER] for m in range(NX)], axis=0)
        states, grads = chain([triple(cin.at[part, m]) for m in range(NC)], state, grad)
        for m in range(NC):
            cdo[part, m, 0] = states[m]
            cdo[part, m, 1] = grads[m]
        cdcopy(part).start()

    def down_z(part):
        def one(core, state, grad):
            states, grads = chain([triple(zin.at[part, m, core]) for m in range(NZ)], state, grad)
            for m in range(NZ):
                zdo[part, m, core, 0] = states[m]
                zdo[part, m, core, 1] = grads[m]

        one(c, cdo[part, c, 0], cdo[part, c, 1])
        for d in (2, 1, 3):
            zdcopy(d, part, 0).start()
        cdcopy(part).wait_recv()
        one(oc, cdi[part, 0], cdi[part, 1])
        for d in (2, 1, 3):
            zdcopy(d, part, 1).start()
        sgin[part, z] = zdo[part, z]

    pl.semaphore_wait(barrier, len(peers))

    def up(i, _):
        d, part = place(i)
        zz = zpeer(d)
        slot = 2 * zz + part

        @pl.when(part == 0)
        def _():
            for copy in rows_of(zz):
                copy.wait()

        for copy in values_of(zz, part):
            copy.wait()
        phase1(qb.at[zz], kb.at[zz], vb.at[slot], gob.at[slot], ldp.at[slot], blp.at[slot], tri.at[slot],
               t_ref.at[slot], m_ref.at[slot], gam_ref.at[slot], u_ref.at[slot], w_ref.at[slot], r_ref.at[slot],
               aux_ref.at[slot], end_ref.at[slot])

        @pl.when(lax.rem(i, NZ) < NZ - 1)
        def _():
            zcopy(d, part).start()

        for step, stage in UP_STAGES:
            @pl.when(i == step)
            def _():
                stage_of[stage](0)

        return 0

    stage_of = dict(z=join_z, core=join_core, x=join_x, dx=down_x, dcore=down_core, dz=down_z)
    lax.fori_loop(0, NZ * PARTS, up, 0)
    for stage, part in MIDDLE:
        stage_of[stage](part)

    def down(i, _):
        d, part = place(lax.rem(i, NZ) + NZ - 1)
        part = lax.div(i, NZ)
        for step, stage in DOWN_STAGES:
            @pl.when(i == step)
            def _():
                stage_of[stage](1)

        @pl.when(lax.rem(i, NZ) > 0)
        def _():
            zdcopy(d, part, 0).wait_recv()
            zdcopy(d, part, 1).wait_recv()

        zz = lax.rem(z + NZ - d, NZ)
        slot = 2 * zz + part
        phase3(part, qb.at[zz], kb.at[zz], vb.at[slot], gob.at[slot], blp.at[slot], sgin.at[part, zz],
               t_ref.at[slot], m_ref.at[slot], gam_ref.at[slot], u_ref.at[slot], w_ref.at[slot], r_ref.at[slot],
               aux_ref.at[slot], end_ref.at[slot],
               outb.at[slot], gqb.at[zz], gkb.at[zz], gvb.at[slot], gdp.at[slot], gbp.at[slot])
        for copy in outputs_of(zz, part):
            copy.start()

        @pl.when(part == PARTS - 1)
        def _():
            for copy in grads_of(zz):
                copy.start()

        return 0

    lax.fori_loop(0, NZ * PARTS, down, 0)
    for zz in range(NZ):
        for part in range(PARTS):
            for j in range(2):
                h = SHARE * zz + 2 * j + part
                gd_ref[h : h + 1] = gdp[2 * zz + part, j : j + 1]
                gb_ref[h : h + 1] = gbp[2 * zz + part, j : j + 1]

    for part in range(PARTS):
        for d in range(1, NZ):
            zcopy(d, part).wait_send()
            zdcopy(d, part, 0).wait_send()
            zdcopy(d, part, 1).wait_send()
            xcopy(d, part).wait_send()
            xdcopy(d, part).wait_send()
            ycopy(d, part).wait_send()
        ccopy(part).wait_send()
        cdcopy(part).wait_send()

    def store_wait(zz, _):
        for copy in grads_of(zz):
            copy.wait()
        for part in range(PARTS):
            for copy in outputs_of(zz, part):
                copy.wait()
        return 0

    lax.fori_loop(0, NZ, store_wait, 0)


UP_STAGES = ((5, "z"), (6, "core"), (7, "x"))
MIDDLE = (("dx", 0), ("z", 1), ("core", 1), ("dcore", 0), ("dz", 0), ("x", 1))
DOWN_STAGES = ((1, "dx"), (2, "dcore"), (2, "dz"))


def run_layer(q, k, v, go, ld, bl):
    dma = pltpu.SemaphoreType.DMA

    def vm(*shape, dtype=F32):
        return pltpu.VMEM(shape, dtype)

    hbm = pl.BlockSpec(memory_space=pl.ANY)
    vmem = pl.BlockSpec(memory_space=pltpu.VMEM)
    slots = NZ * PARTS
    piece = D + 2 * QUARTER
    return pl.pallas_call(
        layer_kernel,
        in_specs=[hbm] * 4 + [vmem] * 2,
        out_specs=[hbm] * 4 + [vmem] * 2,
        out_shape=[
            jax.ShapeDtypeStruct((TOK, HEADS * D), F32),
            jax.ShapeDtypeStruct((TOK, KHEADS * D), F32),
            jax.ShapeDtypeStruct((TOK, KHEADS * D), F32),
            jax.ShapeDtypeStruct((TOK, HEADS * D), F32),
            jax.ShapeDtypeStruct((HEADS, TOK), F32),
            jax.ShapeDtypeStruct((HEADS, TOK), F32),
        ],
        scratch_shapes=[
            vm(NZ, TOK, 2 * D, dtype=BF16), vm(NZ, TOK, 2 * D, dtype=BF16),
            vm(slots, 2, TOK, D, dtype=BF16), vm(slots, 2, TOK, D, dtype=BF16),
            vm(slots, 2, TOK), vm(slots, 2, TOK), vm(slots, 2, TOK), vm(slots, 2, TOK),
            vm(slots, 2, 2, TOK, TOK, dtype=BF16), vm(slots, 2, 2, TOK, TOK, dtype=BF16), vm(slots, 2, TOK, TOK),
            vm(slots, 2, TOK, D), vm(slots, 2, 2, TOK, D, dtype=BF16), vm(slots, 2, D, TOK),
            vm(slots, TOK, D), vm(slots, 2, 8, D),
            vm(slots, NC, 3, D, D), vm(PARTS, NZ, NC, 3, D, D),
            vm(PARTS, 3, D, D), vm(PARTS, NC, 3, D, D),
            vm(PARTS, NX, piece, D), vm(PARTS, NX, piece, D), vm(PARTS, NY, piece, D),
            vm(PARTS, NX, 2 * QUARTER, D), vm(PARTS, NX, 2 * QUARTER, D),
            vm(PARTS, NC, 2, D, D), vm(PARTS, 2, D, D),
            vm(PARTS, NZ, NC, 2, D, D), vm(PARTS, NZ, NC, 2, D, D),
            vm(slots, 2, TOK, D), vm(NZ, TOK, 2 * D), vm(NZ, TOK, 2 * D), vm(slots, 2, TOK, D),
            dma((6, slots)), dma((6, slots)),
            dma((NZ - 1, PARTS)), dma((NZ - 1, PARTS)), dma((PARTS,)), dma((PARTS,)),
            dma((NX - 1, PARTS)), dma((NX - 1, PARTS)), dma((NY - 1, PARTS)), dma((NY - 1, PARTS)),
            dma((NX - 1, PARTS)), dma((NX - 1, PARTS)), dma((PARTS,)), dma((PARTS,)),
            dma((NZ - 1, NC * PARTS)), dma((NZ - 1, NC * PARTS)),
        ],
        compiler_params=pltpu.CompilerParams(
            collective_id=0, has_side_effects=True, vmem_limit_bytes=VMEM_LIMIT),
        name="delta_layer",
    )(q, k, v, go, ld, bl)


def on_device(query_rows, key_rows, value_rows, log_decay, beta_logit, grad_out):
    return tuple(run_layer(query_rows, key_rows, value_rows, grad_out, log_decay, beta_logit))


def solution(mesh):
    rows = P(("ctx", "grp"), None)
    heads = P(None, ("ctx", "grp"))
    return jax.shard_map(
        on_device,
        mesh=mesh,
        in_specs=(rows, rows, rows, heads, heads, rows),
        out_specs=(rows, rows, rows, rows, heads, heads),
        check_vma=False,
    )
```

time: 119 us -> 101 us (0.85)
  Pallas kernels: 106 us -> 92.1 us
  local copies, waits for them, and re-layouts: 12 us -> 7.84 us
    pallas_call x1, Pallas kernels: 106 us -> 92.1 us  [run_layer(): pl.pallas_call(layer_kernel, in_specs=[hbm] * 4 + [vmem] * 2, out_specs=[...]
    reshape x4 -> x0, local copies, waits for them, and re-layouts: 5.34 us -> none  [the longest x2 2.67 us: run_layer(): return (*outs, gd.reshape(HEADS, TOK), gb.reshape(HEADS, TOK))]
    unnamed x10 -> x16, local copies, waits for them, and re-layouts: 6.62 us -> 7.84 us
where the time goes in v3:
time: 101 us
  Pallas kernels  92.1 us (91%)
  local copies, waits for them, and re-layouts  7.84 us (8%)
    pallas_call x1, Pallas kernels, run_layer(): pl.pallas_call(layer_kernel, in_specs=[hbm] * 4 + [vmem] * 2, out_specs=[...  92.1 us
    unnamed x16, local copies, waits for them, and re-layouts  7.84 us

profile of v3, /device:TPU:0, one launch (start us, length us, event | category | flops | bytes accessed | tf_op | source)
XLA Modules:
  0.0 100.6 jit_solution(17512052087929073022)
XLA Ops:
  0.6 92.1 %delta_layer.1 = (f32[256,2048]{1,0:T(8,128)}, f32[256,1024]{1,0:T(8,128)}, f32[256,1024]{1,0:T(8,128)}, f32[256,2048]{1,0:T(8,128)}, f32[16,256]{1,0:T(8,128)}, /*index=5*/f32[16,256]{1,0:T(8,128)}) custom-call(bf16[256,1024]{1,0:T(8,128)(2,1)} %q_hbm.1, bf16[256,1024]{1,0:T(8,128)(2,1)} %k_hbm.1, bf16[256,2048]{1,0:T(8,128)(2,1)} %v_hbm.1, ...), custom_call_target="tpu_custom_call" | custom-call | tf_op jit(solution)/shard_map/delta_layer/pallas_call | solution.py:611
  92.8 0.0 copy-start.2
  92.8 0.0 copy-start.1
  92.8 3.3 %copy.18 = f32[256,2048]{1,0:T(8,128)} copy(f32[256,2048]{1,0:T(8,128)} %get-tuple-element.12) | data formatting | bytes 4194304
  96.1 0.0 copy-done.2
  96.1 0.0 copy-start
  96.1 1.0 copy.19
  97.0 0.0 copy-done.1
  97.0 1.0 copy.20
  98.0 0.1 copy-done
  98.1 0.0 copy-start.4
  98.1 0.0 copy-start.3
  98.1 1.3 %copy.21 = f32[256,2048]{1,0:T(8,128)} copy(f32[256,2048]{1,0:T(8,128)S(1)} %copy-done) | data formatting | bytes 4194304
  99.4 0.0 copy-done.4
  99.4 0.6 copy.22
  100.0 0.0 copy-done.3
  100.0 0.6 copy.23
Async XLA Ops:
  92.8 3.3 %copy-start.2 = (f32[256,1024]{1,0:T(8,128)S(1)}, f32[256,1024]{1,0:T(8,128)}, u32[]{:S(2)}) copy-start(f32[256,1024]{1,0:T(8,128)} %get-tuple-element.13) | copy-start | bytes 3145732
  92.8 4.3 %copy-start.1 = (f32[256,1024]{1,0:T(8,128)S(1)}, f32[256,1024]{1,0:T(8,128)}, u32[]{:S(2)}) copy-start(f32[256,1024]{1,0:T(8,128)} %get-tuple-element.14) | copy-start | bytes 3145732
  96.1 2.0 %copy-start = (f32[256,2048]{1,0:T(8,128)S(1)}, f32[256,2048]{1,0:T(8,128)}, u32[]{:S(2)}) copy-start(f32[256,2048]{1,0:T(8,128)} %get-tuple-element.15) | copy-start | bytes 6291460
  98.1 1.3 %copy-start.4 = (f32[16,256]{1,0:T(8,128)S(1)}, f32[16,256]{1,0:T(8,128)}, u32[]{:S(2)}) copy-start(f32[16,256]{1,0:T(8,128)} %get-tuple-element.16) | copy-start | bytes 49156
  98.1 1.9 %copy-start.3 = (f32[16,256]{1,0:T(8,128)S(1)}, f32[16,256]{1,0:T(8,128)}, u32[]{:S(2)}) copy-start(f32[16,256]{1,0:T(8,128)} %get-tuple-element.17) | copy-start | bytes 49156

commit v4 on v3

--- a/solution.py
+++ b/solution.py
@@ -266,30 +266,32 @@
 QUARTER = D // NX
 
 
-def join(early, late):
-    ae, be, ce = early
-    al, bl, cl = late
-    als = split(al)
-    cls = split(cl)
-    left = (jnp.concatenate([als[0], cls[0]], axis=0), jnp.concatenate([als[1], cls[1]], axis=0))
-    both = dot4(left, split(ae), 1, 0)
-    return both[:D], dot4(split(be), als, 1, 1) + bl, both[D:] + ce
-
-
 def join_all(parts):
     while len(parts) > 1:
-        parts = [join(parts[i], parts[i + 1]) for i in range(0, len(parts), 2)]
+        early, late = parts[0::2], parts[1::2]
+        n = range(len(early))
+        late_a = [split(p[0]) for p in late]
+        late_c = [split(p[2]) for p in late]
+        early_a = [split(p[0]) for p in early]
+        early_b = [split(p[1]) for p in early]
+        left = [[jnp.concatenate([a, g], axis=0) for a, g in zip(late_a[i], late_c[i])] for i in n]
+        down = [dot4(left[i], early_a[i], 1, 0) for i in n]
+        up = [dot4(early_b[i], late_a[i], 1, 1) for i in n]
+        parts = [(down[i][:D], up[i] + late[i][1], down[i][D:] + early[i][2]) for i in n]
     return parts[0]
 
 
 def chain(parts, state, grad):
     split_a = [split(p[0]) for p in parts]
+    n = len(parts)
     states = [state]
-    for i in range(len(parts) - 1):
-        states.append(dot4(split(states[-1]), split_a[i], 1, 1) + parts[i][1])
     grads = [grad]
-    for i in range(len(parts) - 1, 0, -1):
-        grads.append(dot4(split(grads[-1]), split_a[i], 1, 0) + parts[i][2])
+    for i in range(n - 1):
+        ss, gs = split(states[-1]), split(grads[-1])
+        moved = dot4(ss, split_a[i], 1, 1)
+        back = dot4(gs, split_a[n - 1 - i], 1, 0)
+        states.append(moved + parts[i][1])
+        grads.append(back + parts[n - 1 - i][2])
     return states, grads[::-1]
 
 
@@ -500,8 +502,6 @@
             zdcopy(d, part, 1).start()
         sgin[part, z] = zdo[part, z]
 
-    pl.semaphore_wait(barrier, len(peers))
-
     def up(i, _):
         d, part = place(i)
         zz = zpeer(d)
@@ -517,6 +517,10 @@
         phase1(qb.at[zz], kb.at[zz], vb.at[slot], gob.at[slot], ldp.at[slot], blp.at[slot], tri.at[slot],
                t_ref.at[slot], m_ref.at[slot], gam_ref.at[slot], u_ref.at[slot], w_ref.at[slot], r_ref.at[slot],
                aux_ref.at[slot], end_ref.at[slot])
+
+        @pl.when(i == 0)
+        def _():
+            pl.semaphore_wait(barrier, len(peers))
 
         @pl.when(lax.rem(i, NZ) < NZ - 1)
         def _():
@@ -646,8 +650,29 @@
     )(q, k, v, go, ld, bl)
 
 
+def hand_over(*refs):
+    n = len(refs) // 2
+    for i in range(n):
+        refs[n + i][...] = refs[i][...]
+
+
+def run_hand_over(arrays):
+    steps = 4
+    specs = [pl.BlockSpec((TOK // steps, a.shape[1]), lambda i: (i, 0)) for a in arrays[:4]]
+    specs += [pl.BlockSpec((HEADS, TOK), lambda i: (0, 0))] * 2
+    return pl.pallas_call(
+        hand_over,
+        grid=(steps,),
+        in_specs=specs,
+        out_specs=specs,
+        out_shape=[jax.ShapeDtypeStruct(a.shape, a.dtype) for a in arrays],
+        compiler_params=pltpu.CompilerParams(vmem_limit_bytes=VMEM_LIMIT),
+        name="results",
+    )(*arrays)
+
+
 def on_device(query_rows, key_rows, value_rows, log_decay, beta_logit, grad_out):
-    return tuple(run_layer(query_rows, key_rows, value_rows, grad_out, log_decay, beta_logit))
+    return tuple(run_hand_over(run_layer(query_rows, key_rows, value_rows, grad_out, log_decay, beta_logit)))
 
 
 def solution(mesh):

time: 101 us -> 95.9 us (0.950)
  local copies, waits for them, and re-layouts: 7.84 us -> 0 us
  Pallas kernels: 92.1 us -> 95 us
    unnamed x16 -> x0, local copies, waits for them, and re-layouts: 7.84 us -> none
    pallas_call x0 -> x1, Pallas kernels: none -> 5.85 us  [run_hand_over(): pl.pallas_call(hand_over, grid=(steps,), in_specs=specs, out_specs=specs,...]
    pallas_call x1, Pallas kernels: 92.1 us -> 89.1 us  [run_layer(): pl.pallas_call(layer_kernel, in_specs=[hbm] * 4 + [vmem] * 2, out_specs=[...]
where the time goes in v4:
time: 95.9 us; the launch traced here: 95.6 us
  Pallas kernels  95 us (99%)
    pallas_call x1, Pallas kernels, run_layer(): pl.pallas_call(layer_kernel, in_specs=[hbm] * 4 + [vmem] * 2, out_specs=[...  89.1 us
    pallas_call x1, Pallas kernels, run_hand_over(): pl.pallas_call(hand_over, grid=(steps,), in_specs=specs, out_specs=specs,...  5.85 us

profile of v4, /device:TPU:0, one launch (start us, length us, event | category | flops | bytes accessed | tf_op | source)
XLA Modules:
  0.0 95.6 jit_solution(8743986392189818948)
XLA Ops:
  0.6 89.1 %delta_layer.1 = (f32[256,2048]{1,0:T(8,128)}, f32[256,1024]{1,0:T(8,128)}, f32[256,1024]{1,0:T(8,128)}, f32[256,2048]{1,0:T(8,128)}, f32[16,256]{1,0:T(8,128)}, /*index=5*/f32[16,256]{1,0:T(8,128)}) custom-call(bf16[256,1024]{1,0:T(8,128)(2,1)} %q_hbm.1, bf16[256,1024]{1,0:T(8,128)(2,1)} %k_hbm.1, bf16[256,2048]{1,0:T(8,128)(2,1)} %v_hbm.1, ...), custom_call_target="tpu_custom_call" | custom-call | tf_op jit(solution)/shard_map/delta_layer/pallas_call | solution.py:615
  89.8 5.9 %results.1 = (f32[256,2048]{1,0:T(8,128)}, f32[256,1024]{1,0:T(8,128)}, f32[256,1024]{1,0:T(8,128)}, f32[256,2048]{1,0:T(8,128)}, f32[16,256]{1,0:T(8,128)}, /*index=5*/f32[16,256]{1,0:T(8,128)}) custom-call(f32[256,2048]{1,0:T(8,128)} %get-tuple-element.12.refs_0_, f32[256,1024]{1,0:T(8,128)} %get-tuple-element.13.refs_1_, ...), custom_call_target="tpu_custom_call" | custom-call | tf_op jit(solution)/shard_map/results/pallas_call | solution.py:663

commit v5 on v4

--- a/solution.py
+++ b/solution.py
@@ -598,7 +598,7 @@
 
 
 UP_STAGES = ((5, "z"), (6, "core"), (7, "x"))
-MIDDLE = (("dx", 0), ("z", 1), ("core", 1), ("dcore", 0), ("dz", 0), ("x", 1))
+MIDDLE = (("dx", 0), ("z", 1), ("dcore", 0), ("core", 1), ("dz", 0), ("x", 1))
 DOWN_STAGES = ((1, "dx"), (2, "dcore"), (2, "dz"))
 
 
@@ -657,7 +657,7 @@
 
 
 def run_hand_over(arrays):
-    steps = 4
+    steps = 2
     specs = [pl.BlockSpec((TOK // steps, a.shape[1]), lambda i: (i, 0)) for a in arrays[:4]]
     specs += [pl.BlockSpec((HEADS, TOK), lambda i: (0, 0))] * 2
     return pl.pallas_call(

time: 95.9 us -> 94.6 us (0.986)
  Pallas kernels: 95 us -> 93.5 us
    pallas_call x1, Pallas kernels: 5.85 us -> 4.78 us  [run_hand_over(): pl.pallas_call(hand_over, grid=(steps,), in_specs=specs, out_specs=specs,...]
where the time goes in v5:
time: 94.6 us; the launch traced here: 94.1 us
  Pallas kernels  93.5 us (99%)
    pallas_call x1, Pallas kernels, run_layer(): pl.pallas_call(layer_kernel, in_specs=[hbm] * 4 + [vmem] * 2, out_specs=[...  88.7 us
    pallas_call x1, Pallas kernels, run_hand_over(): pl.pallas_call(hand_over, grid=(steps,), in_specs=specs, out_specs=specs,...  4.78 us

profile of v5, /device:TPU:0, one launch (start us, length us, event | category | flops | bytes accessed | tf_op | source)
XLA Modules:
  0.0 94.1 jit_solution(1995874491996310051)
XLA Ops:
  0.6 88.7 %delta_layer.1 = (f32[256,2048]{1,0:T(8,128)}, f32[256,1024]{1,0:T(8,128)}, f32[256,1024]{1,0:T(8,128)}, f32[256,2048]{1,0:T(8,128)}, f32[16,256]{1,0:T(8,128)}, /*index=5*/f32[16,256]{1,0:T(8,128)}) custom-call(bf16[256,1024]{1,0:T(8,128)(2,1)} %q_hbm.1, bf16[256,1024]{1,0:T(8,128)(2,1)} %k_hbm.1, bf16[256,2048]{1,0:T(8,128)(2,1)} %v_hbm.1, ...), custom_call_target="tpu_custom_call" | custom-call | tf_op jit(solution)/shard_map/delta_layer/pallas_call | solution.py:615
  89.4 4.8 %results.1 = (f32[256,2048]{1,0:T(8,128)}, f32[256,1024]{1,0:T(8,128)}, f32[256,1024]{1,0:T(8,128)}, f32[256,2048]{1,0:T(8,128)}, f32[16,256]{1,0:T(8,128)}, /*index=5*/f32[16,256]{1,0:T(8,128)}) custom-call(f32[256,2048]{1,0:T(8,128)} %get-tuple-element.12.refs_0_, f32[256,1024]{1,0:T(8,128)} %get-tuple-element.13.refs_1_, ...), custom_call_target="tpu_custom_call" | custom-call | tf_op jit(solution)/shard_map/results/pallas_call | solution.py:663
